TPU v7x, 256 devices: a whole 4x4x8 slice. The times are simulated.
256 devices in a mesh: tm: 8 (over y, x_lo), cam: 16 (over z, core), head: 2 (over x_hi).
Axes of the slice: x: 4 (x_hi: 2, x_lo: 2; x = x_hi * 2 + x_lo), y: 4, z: 8, core: 2. Of those that a mesh axis runs over, the one named last changes fastest.
Arguments:
- tokens: bfloat16 [16, 128, 32, 2048], P('tm', 'cam'), may hold values from -40 to 40
- w_qkv: bfloat16 [2048, 3, 1024], P(None, None, 'head'), may hold values from -0.25 to 0.25
- w_out: bfloat16 [1024, 2048], P('head'), may hold values from -0.1875 to 0.1875
- window_len: int32 [8], P('head'), may hold values from 1 to 4, as said below
- edge_counts: int32 [16], replicated, may hold values from 1 to 8, as said below
- context_kv: bfloat16 [3, 128, 32, 2, 1024], P(None, 'cam', None, None, 'head'), may hold values from -6 to 6
Outputs:
- mixed: bfloat16 [16, 128, 32, 2048], P('tm', 'cam', None, 'head')
Inputs may be any that keep to these rules, and one draw needn't show every extreme that they name: `window_len`: some head has 4 frames and some head 1 frame. `edge_counts`: some boundary shares 8 columns and some 1 column.
All inputs are finite; a program needn't handle non-finite values.
Results may differ from a plain program's by a relative error of at most 0.008.
Values may be sent and summed in bfloat16 or wider, within the bound.
No kernel may reach another device: no remote copies, remote signals or barrier semaphores. Data moves between devices by JAX's collectives and lax.ppermute only.
A program may use at most 128 MiB of HBM per device.

v0:
```python
import functools

import jax
import jax.numpy as jnp
from jax import lax
from jax.experimental import pallas as pl
from jax.experimental.pallas import tpu as pltpu
from jax.sharding import PartitionSpec as P

AXES = ("tm", "cam", "head")
HD = 128
WMAX = 4
PAIR = 2
TILE = 256
LOG2E = 1.4426950408889634
MIB = 1 << 20
ANY = pl.BlockSpec(memory_space=pl.ANY)
VMEM = pl.BlockSpec(memory_space=pltpu.VMEM)
SMEM = pl.BlockSpec(memory_space=pltpu.SMEM)
PARAMS = pltpu.CompilerParams(vmem_limit_bytes=64 * MIB)
SMALL = pl.CostEstimate(flops=1000, bytes_accessed=1000, transcendentals=0)


def cost(us):
    return pl.CostEstimate(flops=int(us * 1.15e9), bytes_accessed=1000, transcendentals=0)


C_SEND, C_OWN, C_GATHER, C_ATTEND, C_MIX = 1, 1, 2, 1, 1
SPLIT, CTX_FIRST, Q_AFTER, OUTER_B, W_AFTER, EXCH = 0, 1, 2, 1, 1, 0


def pairs_of(sizes, move):
    tm, cam, head = sizes
    flat = lambda t, c, h: (t * cam + c) * head + h
    return [
        (flat(t, c, h), flat(*move(t, c, h)))
        for t in range(tm)
        for c in range(cam)
        for h in range(head)
    ]


def x_low():
    return lax.axis_index("tm") % 2


def bf16(*shape):
    return jax.ShapeDtypeStruct(shape, jnp.bfloat16)


def project_kernel(blocks, chunks, tokens, w3, *refs):
    outs, (flat, w, sem_t, sem_w) = refs[:-4], refs[-4:]
    mine = x_low()
    depth = flat.shape[1] // chunks
    steps = []
    for k in range(chunks):
        ks = pl.ds(k * depth, depth)
        copies = [pltpu.make_async_copy(tokens.at[:, ks], flat.at[:, ks], sem_t.at[k])]
        for i, (which, own, _, _) in enumerate(blocks):
            col = pl.multiple_of(PAIR * HD * (mine if own else 1 - mine), PAIR * HD)
            copies.append(
                pltpu.make_async_copy(
                    w3.at[which, ks, pl.ds(col, PAIR * HD)],
                    w.at[ks, pl.ds(i * PAIR * HD, PAIR * HD)],
                    sem_w.at[k, i],
                )
            )
        steps.append(copies)
        for copy in copies:
            copy.start()
    total = None
    for k, copies in enumerate(steps):
        for copy in copies:
            copy.wait()
        ks = slice(k * depth, (k + 1) * depth)
        made = jnp.dot(flat[:, ks], w[ks, :], preferred_element_type=jnp.float32)
        total = made if total is None else total + made
    total = total.astype(jnp.bfloat16)
    for i, (_, _, out, at) in enumerate(blocks):
        for head in range(PAIR):
            col = (i * PAIR + head) * HD
            piece = total[:, col : col + HD].reshape(-1, TILE, HD)
            if at:
                outs[out + head][(0,) + at] = piece
            else:
                outs[out][head] = piece


def project(blocks, shapes, tokens, w3, estimate):
    rows, width = tokens.shape
    chunks = 4
    return pl.pallas_call(
        functools.partial(project_kernel, blocks, chunks),
        out_shape=shapes,
        in_specs=[ANY, ANY],
        out_specs=[VMEM] * len(shapes),
        scratch_shapes=[
            pltpu.VMEM((rows, width), jnp.bfloat16),
            pltpu.VMEM((width, len(blocks) * PAIR * HD), jnp.bfloat16),
            pltpu.SemaphoreType.DMA((chunks,)),
            pltpu.SemaphoreType.DMA((chunks, len(blocks))),
        ],
        compiler_params=PARAMS,
        cost_estimate=estimate,
    )(tokens, w3)


def run_copies(pairs, sems):
    copies = [pltpu.make_async_copy(src, dst, sems.at[i]) for i, (src, dst) in enumerate(pairs)]
    for copy in copies:
        copy.start()
    for copy in copies:
        copy.wait()


def gather_kernel(kvx, kvm, ctx, four, halo, sems):
    tm, count = lax.axis_index("tm"), lax.axis_size("tm")
    mine = tm % 2
    pairs = [(kvm, four.at[:, pl.ds(2 * mine, 2)]), (kvx, four.at[:, pl.ds(2 - 2 * mine, 2)])]

    @pl.when(tm >= count - 2)
    def _():
        run_copies(pairs + [(ctx, halo)], sems)

    @pl.when((tm < count - 2) & (mine == 0))
    def _():
        run_copies(pairs + [(kvm.at[:, 1], halo.at[:, 0]), (kvx, halo.at[:, pl.ds(1, 2)])], sems)

    @pl.when((tm < count - 2) & (mine == 1))
    def _():
        run_copies(pairs + [(kvx.at[:, 1], halo.at[:, 0]), (kvm, halo.at[:, pl.ds(1, 2)])], sems)


def gather(kvx, kvm, ctx):
    return pl.pallas_call(
        gather_kernel,
        out_shape=[bf16(2, 4, TILE, HD), bf16(2, 3, TILE, HD)],
        in_specs=[ANY] * 3,
        out_specs=[VMEM] * 2,
        scratch_shapes=[pltpu.SemaphoreType.DMA((4,))],
        compiler_params=PARAMS,
        cost_estimate=cost(C_GATHER),
    )(kvx, kvm, ctx)


def attend_pairs(plan, count, off, bias, q, keys, values, peak, acc, bufs, at_step=None):
    score_a, score_b, weight_a, weight_b = bufs
    scale = LOG2E / HD**0.5

    def scored(i, scores):
        scores[...] = lax.dot_general(
            q[plan[0, i]], keys[plan[1, i]], (((1,), (1,)), ((), ())), preferred_element_type=jnp.float32
        )

    def weighed(i, scores, weights):
        at = plan[0, i]
        here = scores[...] * scale + (bias + off[i])
        old = peak[at]
        new = jnp.maximum(old, jnp.max(here, axis=1, keepdims=True))
        weights[...] = jnp.exp2(here - new[:, :1]).astype(jnp.bfloat16)
        shrink = jnp.exp2(old - new)
        peak[at] = new
        acc[at] = acc[at] * jnp.concatenate([shrink, shrink], axis=1)

    def added(i, weights):
        at = plan[0, i]
        acc[at] = acc[at] + jnp.dot(weights[...], values[plan[1, i]], preferred_element_type=jnp.float32)

    scored(0, score_a)
    weighed(0, score_a, weight_a)
    scored(1, score_b)

    def step(j, carry):
        if at_step is not None:
            at_step(j)
        i = 2 * j
        scored(i + 2, score_a)
        weighed(i + 1, score_b, weight_b)
        added(i, weight_a)
        scored(i + 3, score_b)
        weighed(i + 2, score_a, weight_a)
        added(i + 1, weight_b)
        return carry

    lax.fori_loop(0, lax.div(count + 1, 2), step, 0)


def plan_pairs(window, plan, off):
    count = 4 * window
    for back in range(WMAX):
        for frame in range(4):
            here = 4 * back + frame
            plan[0, here] = frame
            plan[1, here] = 3 + frame - back
            off[here] = 0.0
    for more in range(3):
        plan[0, count + more] = 0
        plan[1, count + more] = 3
        off[count + more] = -jnp.inf
    return count


def edge_bias(edges):
    cam, count = lax.axis_index("cam"), lax.axis_size("cam")
    left, right = edges[(cam + count - 1) % count], edges[cam]
    spot = lax.broadcasted_iota(jnp.int32, (1, 3 * TILE), 1)
    seen = (spot >= TILE - left * (TILE // 8)) & (spot < 2 * TILE + right * (TILE // 8))
    return jnp.where(seen, 0.0, -jnp.inf).astype(jnp.float32)


def started(pairs, sems):
    copies = [pltpu.make_async_copy(src, dst, sem) for (src, dst), sem in zip(pairs, sems)]
    for copy in copies:
        copy.start()
    return copies


PLACES = (1, 0, 2)


def attend_kernel(head, windows, edges, q_own, q_far, *refs):
    pieces, (out_own, out_far, q, keys, values, peak, acc, *bufs, plan, off, sems) = refs[:6], refs[6:]
    mine = x_low()
    pairs = [(q_own.at[head], q.at[pl.ds(2 * mine, 2)]), (q_far.at[head], q.at[pl.ds(2 - 2 * mine, 2)])]
    for n, (piece, frames) in enumerate(zip(pieces, [pl.ds(3, 4)] * 3 + [pl.ds(0, 3)] * 3)):
        rows = pl.ds(PLACES[n % 3] * TILE, TILE)
        pairs.append((piece.at[0], keys.at[frames, rows]))
        pairs.append((piece.at[1], values.at[frames, rows, pl.ds(0, HD)]))
    copies = started(pairs, [sems.at[i] for i in range(len(pairs))])
    values[:, :, HD:] = jnp.ones((values.shape[0], 3 * TILE, HD), jnp.bfloat16)
    acc[...] = jnp.zeros_like(acc)
    peak[...] = jnp.full_like(peak, -jnp.inf)
    count = plan_pairs(windows[PAIR * mine + head], plan, off)
    for copy in copies[:8]:
        copy.wait()

    def earlier(j):
        @pl.when(j == 1)
        def _():
            for copy in copies[8:]:
                copy.wait()

    attend_pairs(plan, count, off, edge_bias(edges), q, keys, values, peak, acc, bufs, earlier)
    for out, first in ((out_own, 2 * mine), (out_far, 2 - 2 * mine)):
        for n in range(2):
            done = acc[first + n]
            out[n] = (done[:, :HD] / done[:, HD:]).astype(jnp.bfloat16)


def attend(head, windows, edges, q_own, q_far, pieces):
    return pl.pallas_call(
        functools.partial(attend_kernel, head),
        out_shape=[bf16(2, TILE, HD)] * 2,
        in_specs=[SMEM, SMEM] + [ANY] * (2 + len(pieces)),
        out_specs=[VMEM] * 2,
        scratch_shapes=[
            pltpu.VMEM((4, TILE, HD), jnp.bfloat16),
            pltpu.VMEM((7, 3 * TILE, HD), jnp.bfloat16),
            pltpu.VMEM((7, 3 * TILE, 2 * HD), jnp.bfloat16),
            pltpu.VMEM((4, TILE, HD), jnp.float32),
            pltpu.VMEM((4, TILE, 2 * HD), jnp.float32),
            pltpu.VMEM((TILE, 3 * TILE), jnp.float32),
            pltpu.VMEM((TILE, 3 * TILE), jnp.float32),
            pltpu.VMEM((TILE, 3 * TILE), jnp.bfloat16),
            pltpu.VMEM((TILE, 3 * TILE), jnp.bfloat16),
            pltpu.SMEM((2, 4 * WMAX + 4), jnp.int32),
            pltpu.SMEM((4 * WMAX + 4,), jnp.float32),
            pltpu.SemaphoreType.DMA((14,)),
        ],
        compiler_params=PARAMS,
        cost_estimate=cost(C_ATTEND),
    )(windows, edges, q_own, q_far, *pieces)


def mix_kernel(*refs):
    pieces, (w_own, w_mine, w_core, out, held, w, made, sem_a, sem_o) = refs[:8], refs[8:]
    mine, core = x_low(), lax.axis_index("cam") % 2
    part = PAIR * HD
    width = w_own.shape[1]
    half = width // 2
    rows = lambda at: pl.ds(pl.multiple_of(at, part), part)
    inputs = started(
        [(piece, held.at[n % 4, :, :, pl.ds(n // 4 * HD, HD)]) for n, piece in enumerate(pieces)],
        [sem_a.at[i] for i in range(8)],
    )

    @pl.when(core == mine)
    def _():
        w[0], w[1] = w_mine[...], w_core[...]

    @pl.when(core != mine)
    def _():
        w[0], w[1] = w_core[...], w_mine[...]

    for copy in inputs:
        copy.wait()

    def group(first, weights, cols):
        total = None
        for n, weight in enumerate(weights):
            both = held[first + n].reshape(2 * TILE, part)
            term = jnp.dot(both, weight[:, cols], preferred_element_type=jnp.float32)
            total = term if total is None else total + term
        return total.astype(jnp.bfloat16).astype(jnp.float32)

    outs = []
    for n in range(2):
        cols = slice(n * half, (n + 1) * half)
        first = group(0, (w_own.at[rows(part * mine)], w_own.at[rows(part * (1 - mine))]), cols)
        second = group(2, (w.at[0], w.at[1]), cols)
        made[n] = (first + second).astype(jnp.bfloat16)
        outs += started([(made.at[n], out.at[:, pl.ds(n * half, half)])], [sem_o.at[n]])
    for copy in outs:
        copy.wait()


def mix(attended, w_own, w_mine, w_core):
    rows, width = 2 * TILE, w_own.shape[1]
    return pl.pallas_call(
        mix_kernel,
        out_shape=bf16(rows, width),
        in_specs=[ANY] * 8 + [VMEM] * 3,
        out_specs=ANY,
        scratch_shapes=[
            pltpu.VMEM((4, 2, TILE, PAIR * HD), jnp.bfloat16),
            pltpu.VMEM((2,) + w_mine.shape, jnp.bfloat16),
            pltpu.VMEM((2, rows, width // 2), jnp.bfloat16),
            pltpu.SemaphoreType.DMA((8,)),
            pltpu.SemaphoreType.DMA((2,)),
        ],
        compiler_params=pltpu.CompilerParams(vmem_limit_bytes=24 * MIB),
        cost_estimate=cost(C_MIX),
    )(*attended, w_own, w_mine, w_core)


def body(tokens, w_qkv, w_out, window_len, edge_counts, context_kv):
    frames, cols, row_count, width = tokens.shape
    sizes = tuple(lax.axis_size(axis) for axis in AXES)
    tm_count, cam_count, _ = sizes
    tm, cam, x_hi = (lax.axis_index(axis) for axis in AXES)
    x_lo, core = tm % 2, cam % 2

    def moved(move):
        pairs = pairs_of(sizes, move)
        return lambda shard: lax.ppermute(shard, AXES, pairs)

    to_mate = moved(lambda t, c, h: (t ^ 1, c, h))
    to_over = moved(lambda t, c, h: (t, c, 1 - h))
    to_diag = moved(lambda t, c, h: (t ^ 1, c, 1 - h))
    to_later = moved(lambda t, c, h: ((t + 2) % tm_count, c, h))
    to_right = moved(lambda t, c, h: (t, (c + 1) % cam_count, h))
    to_left = moved(lambda t, c, h: (t, (c - 1) % cam_count, h))
    to_core = moved(lambda t, c, h: (t, c ^ 1, h))
    wide = lambda shard: [shard, to_right(shard), to_left(shard)]

    flat = tokens.reshape(frames * cols * row_count, width)
    w3 = jnp.transpose(w_qkv, (1, 0, 2))
    kv_shape = bf16(1, 2, frames, TILE, HD)
    q_shape = bf16(PAIR, frames, TILE, HD)

    sent = project([(1, False, 0, (0,)), (2, False, 0, (1,))], [kv_shape] * 2, flat, w3, cost(C_SEND))
    kvx = [to_mate(one[0]) for one in sent]
    if not SPLIT:
        kvx = lax.optimization_barrier(kvx)

    def cached(context_kv):
        ctx = []
        for head in range(PAIR):
            part = lax.dynamic_slice_in_dim(context_kv, (PAIR * x_lo + head) * HD, HD, 4)
            ctx.append(jnp.transpose(part.reshape(WMAX - 1, TILE, 2, HD), (2, 0, 1, 3)))
        return ctx

    if CTX_FIRST:
        ctx = cached(lax.optimization_barrier((context_kv, sent))[0])
        flat, _ = lax.optimization_barrier((flat, ctx))
    else:
        flat, _ = lax.optimization_barrier((flat, sent))
    *kvm, q_sent, q_own = project(
        [(1, True, 0, (0,)), (2, True, 0, (1,)), (0, False, 2, ()), (0, True, 3, ())],
        [kv_shape] * 2 + [q_shape] * 2,
        flat,
        w3,
        cost(C_OWN),
    )
    if not CTX_FIRST:
        ctx = cached(lax.optimization_barrier((context_kv, q_own))[0])
    if Q_AFTER:
        q_sent, _ = lax.optimization_barrier((q_sent, kvx[Q_AFTER - 1]))
    q_far = to_mate(q_sent)

    four, halo = [], []
    for head in range(PAIR):
        one, later = gather(kvx[head], kvm[head][0], ctx[head])
        outer = one
        if head and OUTER_B == 1:
            outer, q_far, four[0] = lax.optimization_barrier((one, q_far, four[0]))
        if head and OUTER_B == 2:
            outer, halo[0] = lax.optimization_barrier((one, halo[0]))
        four.append([one, to_right(outer), to_left(outer)])
        halo.append(to_later(later))
        if head == 0 or OUTER_B != 3:
            halo[head] = wide(halo[head])
        else:
            later, four = lax.optimization_barrier((halo[1], four))
            halo[1] = wide(later)

    half = w_out.shape[1] // 2

    def fetched(w_out):
        w_part = lax.dynamic_slice(w_out, (core * PAIR * HD, (1 - x_hi) * half), (PAIR * HD, half))
        return to_diag(w_part)

    if W_AFTER == 0:
        w_mine = fetched(w_out)
    if W_AFTER == 1:
        w_mine = fetched(lax.optimization_barrier((w_out, four[1][0]))[0])
    if W_AFTER == 2:
        w_now, four[1] = lax.optimization_barrier((w_out, four[1]))
        w_mine = fetched(w_now)
    if W_AFTER == 3:
        w_now, halo[0] = lax.optimization_barrier((w_out, halo[0]))
        w_mine = fetched(w_now)

    pieces = []
    for head in range(PAIR):
        own, mates = attend(head, window_len, edge_counts, q_own, q_far, four[head] + halo[head])
        if head:
            if EXCH:
                own, mates, pieces = lax.optimization_barrier((own, mates, pieces))
        else:
            if W_AFTER == 4:
                w_mine = fetched(lax.optimization_barrier((w_out, own))[0])
            else:
                w_mine, _ = lax.optimization_barrier((w_mine, own))
            w_core = to_core(w_mine)
            w_own = lax.dynamic_slice_in_dim(lax.optimization_barrier((w_out, own))[0], x_hi * half, half, 1)
        pieces.append([own, to_mate(mates), to_over(own), to_diag(mates)])
    out = mix(pieces[0] + pieces[1], w_own, w_mine, w_core)
    return out.reshape(frames, cols, row_count, -1)


def solution(mesh):
    placed = (
        P("tm", "cam", None, None),
        P(None, None, "head"),
        P("head", None),
        P("head"),
        P(),
        P(None, "cam", None, None, "head"),
    )
    return jax.shard_map(
        body, mesh=mesh, in_specs=placed, out_specs=P("tm", "cam", None, "head"), check_vma=False
    )
```

profile of v0, /device:TPU:1, one launch (start us, length us, event | category | flops | bytes accessed | tf_op | source)
XLA Modules:
  0.0 83.5 jit_solution(3825474549210543231)
XLA Ops:
  0.0 3.8 %shard_map.64 = (bf16[1,2,2,256,128]{4,3,2,1,0:T(8,128)(2,1)}, bf16[1,2,2,256,128]{4,3,2,1,0:T(8,128)(2,1)}) custom-call(bf16[512,2048]{1,0:T(8,128)(2,1)} %bitcast.15, bf16[3,2048,512]{2,1,0:T(8,128)(2,1)} %bitcast.13), custom_call_target="tpu_custom_call" | custom-call | flops 1150000000 | bytes 1000 | tf_op jit(solution)/shard_map/pallas_call | solution.py:92
  3.8 2.1 %collective-permute-start = (bf16[2,2,256,128]{3,2,1,0:T(8,128)(2,1)}, bf16[2,2,256,128]{3,2,1,0:T(8,128)(2,1)}, u32[]{:S(2)}, u32[]{:S(2)}) collective-permute-start(bf16[2,2,256,128]{3,2,1,0:T(8,128)(2,1)} %bitcast.20), channel_id=1, source_target_pairs={{0,32},{1,33},{2,34},{3,35},{4,36},{5,37},{6,38},{7,39},{8,40},{9,... | collective-permute-start | bytes 786440 | tf_op jit(solution)/shard_map/ppermute | solution.py:345
  6.0 2.0 %constant_dynamic-slice_fusion.1 = (bf16[3,8,32,2,128]{4,3,2,1,0:T(2,128)(2,1)S(1)}, bf16[3,8,32,2,128]{4,3,2,1,0:T(2,128)(2,1)S(1)}) fusion(bf16[3,8,32,2,512]{4,3,2,1,0:T(2,128)(2,1)} %param.11, s32[]{:T(128)S(6)} %select_n.28, s32[]{:T(128)S(6)} %select_n.27), kind=kLoop, calls=%fused_computation.1 | loop fusion | bytes 1572872 | tf_op jit(solution)/shard_map/dynamic_slice | solution.py:369
  9.6 5.7 %shard_map.65 = (bf16[1,2,2,256,128]{4,3,2,1,0:T(8,128)(2,1)}, bf16[1,2,2,256,128]{4,3,2,1,0:T(8,128)(2,1)}, bf16[2,2,256,128]{3,2,1,0:T(8,128)(2,1)}, bf16[2,2,256,128]{3,2,1,0:T(8,128)(2,1)}) custom-call(bf16[512,2048]{1,0:T(8,128)(2,1)} %bitcast.16, bf16[3,2048,512]{2,1,0:T(8,128)(2,1)} %bitcast.14), custom_call_target="tpu_custom_call" | custom-call | flops 1150000000 | bytes 1000 | tf_op jit(solution)/shard_map/pallas_call | solution.py:92
  16.5 2.1 %shard_map.67 = (bf16[2,4,256,128]{3,2,1,0:T(8,128)(2,1)}, bf16[2,3,256,128]{3,2,1,0:T(8,128)(2,1)}) custom-call(bf16[2,2,256,128]{3,2,1,0:T(8,128)(2,1)} %collective-permute-done.kvx, bf16[2,2,256,128]{3,2,1,0:T(8,128)(2,1)} %bitcast.22, bf16[2,3,256,128]{3,2,1,0:T(8,128)(2,1)} %bitcast.18), custom_call_target="tpu_custom_call" | custom-call | flops 2300000000 | bytes 1000 | tf_op jit(solution)/shard_map/pallas_call | solution.py:135
  18.6 4.4 %collective-permute-start.3 = (bf16[2,4,256,128]{3,2,1,0:T(8,128)(2,1)}, bf16[2,4,256,128]{3,2,1,0:T(8,128)(2,1)}, u32[]{:S(2)}, u32[]{:S(2)}) collective-permute-start(bf16[2,4,256,128]{3,2,1,0:T(8,128)(2,1)} %get-tuple-element.46.refs_0_), channel_id=1, source_target_pairs={{0,2},{1,3},{2,4},{3,5},{4,6},{5,7},{6,8},{7,9},{8,10},{9,11},{10,... | collective-permute-start | bytes 1572872 | tf_op jit(solution)/shard_map/ppermute | solution.py:345
  23.0 1.3 %collective-permute-start.5 = (bf16[2,3,256,128]{3,2,1,0:T(8,128)(2,1)}, bf16[2,3,256,128]{3,2,1,0:T(8,128)(2,1)}, u32[]{:S(2)}, u32[]{:S(2)}) collective-permute-start(bf16[2,3,256,128]{3,2,1,0:T(8,128)(2,1)} %get-tuple-element.49), channel_id=1, source_target_pairs={{0,64},{1,65},{2,66},{3,67},{4,68},{5,69},{6,70},{7,71},{8,72},{9,... | collective-permute-start | bytes 1179656 | tf_op jit(solution)/shard_map/ppermute | solution.py:345
  25.5 2.1 %shard_map.66 = (bf16[2,4,256,128]{3,2,1,0:T(8,128)(2,1)}, bf16[2,3,256,128]{3,2,1,0:T(8,128)(2,1)}) custom-call(bf16[2,2,256,128]{3,2,1,0:T(8,128)(2,1)} %collective-permute-done.1.kvx, bf16[2,2,256,128]{3,2,1,0:T(8,128)(2,1)} %bitcast.21, bf16[2,3,256,128]{3,2,1,0:T(8,128)(2,1)} %bitcast.17), custom_call_target="tpu_custom_call" | custom-call | flops 2300000000 | bytes 1000 | tf_op jit(solution)/shard_map/pallas_call | solution.py:135
  27.6 1.4 %collective-permute-start.13 = (bf16[2,3,256,128]{3,2,1,0:T(8,128)(2,1)}, bf16[2,3,256,128]{3,2,1,0:T(8,128)(2,1)}, u32[]{:S(2)}, u32[]{:S(2)}) collective-permute-start(bf16[2,3,256,128]{3,2,1,0:T(8,128)(2,1)} %get-tuple-element.53), channel_id=1, source_target_pairs={{0,64},{1,65},{2,66},{3,67},{4,68},{5,69},{6,70},{7,71},{8,72},{9,... | collective-permute-start | bytes 1179656 | tf_op jit(solution)/shard_map/ppermute | solution.py:345
  29.0 5.2 %collective-permute-done.5.refs_3_ = bf16[2,3,256,128]{3,2,1,0:T(8,128)(2,1)} collective-permute-done((bf16[2,3,256,128]{3,2,1,0:T(8,128)(2,1)}, bf16[2,3,256,128]{3,2,1,0:T(8,128)(2,1)}, u32[]{:S(2)}, u32[]{:S(2)}) %collective-permute-start.5) | collective-permute-done | bytes 393248 | tf_op jit(solution)/shard_map/ppermute | solution.py:345
  34.2 1.4 %collective-permute-start.6 = (bf16[2,3,256,128]{3,2,1,0:T(8,128)(2,1)}, bf16[2,3,256,128]{3,2,1,0:T(8,128)(2,1)}, u32[]{:S(2)}, u32[]{:S(2)}) collective-permute-start(bf16[2,3,256,128]{3,2,1,0:T(8,128)(2,1)} %collective-permute-done.5.refs_3_), channel_id=1, source_target_pairs={{0,2},{1,3},{2,4},{3,5},{4,6},{5,7},{6,8},{7,9},{8,10},{9,11},{10,... | collective-permute-start | bytes 1179656 | tf_op jit(solution)/shard_map/ppermute | solution.py:345
  35.5 1.9 %dynamic_slice.15 = bf16[256,1024]{1,0:T(8,128)(2,1)} dynamic-slice(bf16[512,2048]{1,0:T(8,128)(2,1)} %param.8, s32[]{:T(128)S(6)} %select_n.31, s32[]{:T(128)S(6)} %select_n.32), dynamic_slice_sizes={256,1024} | dynamic-slice | bytes 1048580 | tf_op jit(solution)/shard_map/dynamic_slice | solution.py:410
  37.4 2.5 %collective-permute-start.19 = (bf16[256,1024]{1,0:T(8,128)(2,1)}, bf16[256,1024]{1,0:T(8,128)(2,1)}, u32[]{:S(2)}, u32[]{:S(2)}) collective-permute-start(bf16[256,1024]{1,0:T(8,128)(2,1)} %dynamic_slice.15), channel_id=1, source_target_pairs={{0,33},{1,32},{2,35},{3,34},{4,37},{5,36},{6,39},{7,38},{8,41},{9,... | collective-permute-start | bytes 1572872 | tf_op jit(solution)/shard_map/ppermute | solution.py:345
  39.9 2.5 %collective-permute-start.11 = (bf16[2,4,256,128]{3,2,1,0:T(8,128)(2,1)}, bf16[2,4,256,128]{3,2,1,0:T(8,128)(2,1)}, u32[]{:S(2)}, u32[]{:S(2)}) collective-permute-start(bf16[2,4,256,128]{3,2,1,0:T(8,128)(2,1)} %get-tuple-element.52.refs_0_), channel_id=1, source_target_pairs={{0,2},{1,3},{2,4},{3,5},{4,6},{5,7},{6,8},{7,9},{8,10},{9,11},{10,... | collective-permute-start | bytes 1572872 | tf_op jit(solution)/shard_map/ppermute | solution.py:345
  44.2 1.4 %collective-permute-start.15 = (bf16[2,3,256,128]{3,2,1,0:T(8,128)(2,1)}, bf16[2,3,256,128]{3,2,1,0:T(8,128)(2,1)}, u32[]{:S(2)}, u32[]{:S(2)}) collective-permute-start(bf16[2,3,256,128]{3,2,1,0:T(8,128)(2,1)} %collective-permute-done.13.refs_3_), channel_id=1, source_target_pairs={{0,30},{1,31},{2,0},{3,1},{4,2},{5,3},{6,4},{7,5},{8,6},{9,7},{10,... | collective-permute-start | bytes 1179656 | tf_op jit(solution)/shard_map/ppermute | solution.py:345
  45.5 8.8 %shard_map.68 = (bf16[2,256,128]{2,1,0:T(8,128)(2,1)}, bf16[2,256,128]{2,1,0:T(8,128)(2,1)}) custom-call(s32[4]{0:T(128)} %windows.3, s32[16]{0:T(128)} %edges.3, bf16[2,2,256,128]{3,2,1,0:T(8,128)(2,1)} %get-tuple-element.36.q_own, bf16[2,2,256,128]{3,2,1,0:T(8,128)(2,1)} %collective-permute-done.2.q_far, ...), custom_call_target="tpu_custom_call" | custom-call | flops 1150000000 | bytes 1000 | tf_op jit(solution)/shard_map/pallas_call | solution.py:251
  54.3 3.0 %collective-permute-start.20 = (bf16[256,1024]{1,0:T(8,128)(2,1)}, bf16[256,1024]{1,0:T(8,128)(2,1)}, u32[]{:S(2)}, u32[]{:S(2)}) collective-permute-start(bf16[256,1024]{1,0:T(8,128)(2,1)} %collective-permute-done.19.refs_9_), channel_id=1, source_target_pairs={{0,2},{1,3},{2,0},{3,1},{4,6},{5,7},{6,4},{7,5},{8,10},{9,11},{10,... | collective-permute-start | bytes 1572872 | tf_op jit(solution)/shard_map/ppermute | solution.py:345
  58.2 1.6 %collective-permute-start.9 = (bf16[2,256,128]{2,1,0:T(8,128)(2,1)}, bf16[2,256,128]{2,1,0:T(8,128)(2,1)}, u32[]{:S(2)}, u32[]{:S(2)}) collective-permute-start(bf16[2,256,128]{2,1,0:T(8,128)(2,1)} %get-tuple-element.50.refs_0_), channel_id=1, source_target_pairs={{0,1},{1,0},{2,3},{3,2},{4,5},{5,4},{6,7},{7,6},{8,9},{9,8},{10,11... | collective-permute-start | bytes 393224 | tf_op jit(solution)/shard_map/ppermute | solution.py:345
  59.8 1.4 %collective-permute-start.10 = (bf16[2,256,128]{2,1,0:T(8,128)(2,1)}, bf16[2,256,128]{2,1,0:T(8,128)(2,1)}, u32[]{:S(2)}, u32[]{:S(2)}) collective-permute-start(bf16[2,256,128]{2,1,0:T(8,128)(2,1)} %get-tuple-element.51), channel_id=1, source_target_pairs={{0,33},{1,32},{2,35},{3,34},{4,37},{5,36},{6,39},{7,38},{8,41},{9,... | collective-permute-start | bytes 393224 | tf_op jit(solution)/shard_map/ppermute | solution.py:345
  61.2 5.0 %shard_map.69 = (bf16[2,256,128]{2,1,0:T(8,128)(2,1)}, bf16[2,256,128]{2,1,0:T(8,128)(2,1)}) custom-call(s32[4]{0:T(128)} %windows.3, s32[16]{0:T(128)} %edges.3, bf16[2,2,256,128]{3,2,1,0:T(8,128)(2,1)} %get-tuple-element.36.q_own, bf16[2,2,256,128]{3,2,1,0:T(8,128)(2,1)} %collective-permute-done.2.q_far, ...), custom_call_target="tpu_custom_call" | custom-call | flops 1150000000 | bytes 1000 | tf_op jit(solution)/shard_map/pallas_call | solution.py:251
  67.3 4.3 %collective-permute-start.18 = (bf16[2,256,128]{2,1,0:T(8,128)(2,1)}, bf16[2,256,128]{2,1,0:T(8,128)(2,1)S(1)}, u32[]{:S(2)}, u32[]{:S(2)}) collective-permute-start(bf16[2,256,128]{2,1,0:T(8,128)(2,1)} %get-tuple-element.55), channel_id=1, source_target_pairs={{0,33},{1,32},{2,35},{3,34},{4,37},{5,36},{6,39},{7,38},{8,41},{9,... | collective-permute-start | bytes 393224 | tf_op jit(solution)/shard_map/ppermute | solution.py:345
  72.8 1.3 %constant_dynamic-slice_fusion.refs_8_ = bf16[512,1024]{1,0:T(8,128)(2,1)S(1)} fusion(bf16[512,2048]{1,0:T(8,128)(2,1)} %param.8, s32[]{:T(128)S(6)} %select_n.29), kind=kLoop, calls=%fused_computation | loop fusion | bytes 2097156 | tf_op jit(solution)/shard_map/dynamic_slice | solution.py:436
  74.1 4.7 %collective-permute-done.17.refs_6_ = bf16[2,256,128]{2,1,0:T(8,128)(2,1)S(1)} collective-permute-done((bf16[2,256,128]{2,1,0:T(8,128)(2,1)}, bf16[2,256,128]{2,1,0:T(8,128)(2,1)S(1)}, u32[]{:S(2)}, u32[]{:S(2)}) %collective-permute-start.17) | collective-permute-done | bytes 131104 | tf_op jit(solution)/shard_map/ppermute | solution.py:345
  78.9 4.4 %shard_map.70 = bf16[512,1024]{1,0:T(8,128)(2,1)} custom-call(bf16[2,256,128]{2,1,0:T(8,128)(2,1)S(1)} %copy-done, bf16[2,256,128]{2,1,0:T(8,128)(2,1)} %collective-permute-done.8.refs_1_, bf16[2,256,128]{2,1,0:T(8,128)(2,1)} %collective-permute-done.9.refs_2_, bf16[2,256,128]{2,1,0:T(8,128)(2,1)} %collective-permute-done.10.refs_3_, ...), custom_call_target="tpu_custom_call" | custom-call | flops 1150000000 | bytes 1000 | tf_op jit(solution)/shard_map/pallas_call | solution.py:319
  (34 shorter events, 9.0 us)
Async XLA Ops:
  3.8 11.5 %collective-permute-start = (bf16[2,2,256,128]{3,2,1,0:T(8,128)(2,1)}, bf16[2,2,256,128]{3,2,1,0:T(8,128)(2,1)}, u32[]{:S(2)}, u32[]{:S(2)}) collective-permute-start(bf16[2,2,256,128]{3,2,1,0:T(8,128)(2,1)} %bitcast.20), channel_id=1, source_target_pairs={{0,32},{1,33},{2,34},{3,35},{4,36},{5,37},{6,38},{7,39},{8,40},{9,... | collective-permute-start | bytes 786440 | tf_op jit(solution)/shard_map/ppermute | solution.py:345
  5.9 10.6 %collective-permute-start.1 = (bf16[2,2,256,128]{3,2,1,0:T(8,128)(2,1)}, bf16[2,2,256,128]{3,2,1,0:T(8,128)(2,1)}, u32[]{:S(2)}, u32[]{:S(2)}) collective-permute-start(bf16[2,2,256,128]{3,2,1,0:T(8,128)(2,1)} %bitcast.19), channel_id=1, source_target_pairs={{0,32},{1,33},{2,34},{3,35},{4,36},{5,37},{6,38},{7,39},{8,40},{9,... | collective-permute-start | bytes 786440 | tf_op jit(solution)/shard_map/ppermute | solution.py:345
  18.6 18.8 %collective-permute-start.3 = (bf16[2,4,256,128]{3,2,1,0:T(8,128)(2,1)}, bf16[2,4,256,128]{3,2,1,0:T(8,128)(2,1)}, u32[]{:S(2)}, u32[]{:S(2)}) collective-permute-start(bf16[2,4,256,128]{3,2,1,0:T(8,128)(2,1)} %get-tuple-element.46.refs_0_), channel_id=1, source_target_pairs={{0,2},{1,3},{2,4},{3,5},{4,6},{5,7},{6,8},{7,9},{8,10},{9,11},{10,... | collective-permute-start | bytes 1572872 | tf_op jit(solution)/shard_map/ppermute | solution.py:345
  23.0 11.2 %collective-permute-start.5 = (bf16[2,3,256,128]{3,2,1,0:T(8,128)(2,1)}, bf16[2,3,256,128]{3,2,1,0:T(8,128)(2,1)}, u32[]{:S(2)}, u32[]{:S(2)}) collective-permute-start(bf16[2,3,256,128]{3,2,1,0:T(8,128)(2,1)} %get-tuple-element.49), channel_id=1, source_target_pairs={{0,64},{1,65},{2,66},{3,67},{4,68},{5,69},{6,70},{7,71},{8,72},{9,... | collective-permute-start | bytes 1179656 | tf_op jit(solution)/shard_map/ppermute | solution.py:345
  24.3 15.6 %collective-permute-start.4 = (bf16[2,4,256,128]{3,2,1,0:T(8,128)(2,1)}, bf16[2,4,256,128]{3,2,1,0:T(8,128)(2,1)}, u32[]{:S(2)}, u32[]{:S(2)}) collective-permute-start(bf16[2,4,256,128]{3,2,1,0:T(8,128)(2,1)} %get-tuple-element.46.refs_0_), channel_id=1, source_target_pairs={{0,30},{1,31},{2,0},{3,1},{4,2},{5,3},{6,4},{7,5},{8,6},{9,7},{10,... | collective-permute-start | bytes 1572872 | tf_op jit(solution)/shard_map/ppermute | solution.py:345
  24.3 11.3 %collective-permute-start.2 = (bf16[2,2,256,128]{3,2,1,0:T(8,128)(2,1)}, bf16[2,2,256,128]{3,2,1,0:T(8,128)(2,1)}, u32[]{:S(2)}, u32[]{:S(2)}) collective-permute-start(bf16[2,2,256,128]{3,2,1,0:T(8,128)(2,1)} %get-tuple-element.41), channel_id=1, source_target_pairs={{0,32},{1,33},{2,34},{3,35},{4,36},{5,37},{6,38},{7,39},{8,40},{9,... | collective-permute-start | bytes 786440 | tf_op jit(solution)/shard_map/ppermute | solution.py:345
  27.6 14.8 %collective-permute-start.13 = (bf16[2,3,256,128]{3,2,1,0:T(8,128)(2,1)}, bf16[2,3,256,128]{3,2,1,0:T(8,128)(2,1)}, u32[]{:S(2)}, u32[]{:S(2)}) collective-permute-start(bf16[2,3,256,128]{3,2,1,0:T(8,128)(2,1)} %get-tuple-element.53), channel_id=1, source_target_pairs={{0,64},{1,65},{2,66},{3,67},{4,68},{5,69},{6,70},{7,71},{8,72},{9,... | collective-permute-start | bytes 1179656 | tf_op jit(solution)/shard_map/ppermute | solution.py:345
  34.2 9.1 %collective-permute-start.6 = (bf16[2,3,256,128]{3,2,1,0:T(8,128)(2,1)}, bf16[2,3,256,128]{3,2,1,0:T(8,128)(2,1)}, u32[]{:S(2)}, u32[]{:S(2)}) collective-permute-start(bf16[2,3,256,128]{3,2,1,0:T(8,128)(2,1)} %collective-permute-done.5.refs_3_), channel_id=1, source_target_pairs={{0,2},{1,3},{2,4},{3,5},{4,6},{5,7},{6,8},{7,9},{8,10},{9,11},{10,... | collective-permute-start | bytes 1179656 | tf_op jit(solution)/shard_map/ppermute | solution.py:345
  35.5 8.6 %collective-permute-start.7 = (bf16[2,3,256,128]{3,2,1,0:T(8,128)(2,1)}, bf16[2,3,256,128]{3,2,1,0:T(8,128)(2,1)}, u32[]{:S(2)}, u32[]{:S(2)}) collective-permute-start(bf16[2,3,256,128]{3,2,1,0:T(8,128)(2,1)} %collective-permute-done.5.refs_3_), channel_id=1, source_target_pairs={{0,30},{1,31},{2,0},{3,1},{4,2},{5,3},{6,4},{7,5},{8,6},{9,7},{10,... | collective-permute-start | bytes 1179656 | tf_op jit(solution)/shard_map/ppermute | solution.py:345
  37.4 16.9 %collective-permute-start.19 = (bf16[256,1024]{1,0:T(8,128)(2,1)}, bf16[256,1024]{1,0:T(8,128)(2,1)}, u32[]{:S(2)}, u32[]{:S(2)}) collective-permute-start(bf16[256,1024]{1,0:T(8,128)(2,1)} %dynamic_slice.15), channel_id=1, source_target_pairs={{0,33},{1,32},{2,35},{3,34},{4,37},{5,36},{6,39},{7,38},{8,41},{9,... | collective-permute-start | bytes 1572872 | tf_op jit(solution)/shard_map/ppermute | solution.py:345
  39.9 19.9 %collective-permute-start.11 = (bf16[2,4,256,128]{3,2,1,0:T(8,128)(2,1)}, bf16[2,4,256,128]{3,2,1,0:T(8,128)(2,1)}, u32[]{:S(2)}, u32[]{:S(2)}) collective-permute-start(bf16[2,4,256,128]{3,2,1,0:T(8,128)(2,1)} %get-tuple-element.52.refs_0_), channel_id=1, source_target_pairs={{0,2},{1,3},{2,4},{3,5},{4,6},{5,7},{6,8},{7,9},{8,10},{9,11},{10,... | collective-permute-start | bytes 1572872 | tf_op jit(solution)/shard_map/ppermute | solution.py:345
  42.4 18.8 %collective-permute-start.12 = (bf16[2,4,256,128]{3,2,1,0:T(8,128)(2,1)}, bf16[2,4,256,128]{3,2,1,0:T(8,128)(2,1)}, u32[]{:S(2)}, u32[]{:S(2)}) collective-permute-start(bf16[2,4,256,128]{3,2,1,0:T(8,128)(2,1)} %get-tuple-element.52.refs_0_), channel_id=1, source_target_pairs={{0,30},{1,31},{2,0},{3,1},{4,2},{5,3},{6,4},{7,5},{8,6},{9,7},{10,... | collective-permute-start | bytes 1572872 | tf_op jit(solution)/shard_map/ppermute | solution.py:345
  43.3 14.0 %collective-permute-start.14 = (bf16[2,3,256,128]{3,2,1,0:T(8,128)(2,1)}, bf16[2,3,256,128]{3,2,1,0:T(8,128)(2,1)}, u32[]{:S(2)}, u32[]{:S(2)}) collective-permute-start(bf16[2,3,256,128]{3,2,1,0:T(8,128)(2,1)} %collective-permute-done.13.refs_3_), channel_id=1, source_target_pairs={{0,2},{1,3},{2,4},{3,5},{4,6},{5,7},{6,8},{7,9},{8,10},{9,11},{10,... | collective-permute-start | bytes 1179656 | tf_op jit(solution)/shard_map/ppermute | solution.py:345
  44.2 14.0 %collective-permute-start.15 = (bf16[2,3,256,128]{3,2,1,0:T(8,128)(2,1)}, bf16[2,3,256,128]{3,2,1,0:T(8,128)(2,1)}, u32[]{:S(2)}, u32[]{:S(2)}) collective-permute-start(bf16[2,3,256,128]{3,2,1,0:T(8,128)(2,1)} %collective-permute-done.13.refs_3_), channel_id=1, source_target_pairs={{0,30},{1,31},{2,0},{3,1},{4,2},{5,3},{6,4},{7,5},{8,6},{9,7},{10,... | collective-permute-start | bytes 1179656 | tf_op jit(solution)/shard_map/ppermute | solution.py:345
  54.3 24.6 %collective-permute-start.20 = (bf16[256,1024]{1,0:T(8,128)(2,1)}, bf16[256,1024]{1,0:T(8,128)(2,1)}, u32[]{:S(2)}, u32[]{:S(2)}) collective-permute-start(bf16[256,1024]{1,0:T(8,128)(2,1)} %collective-permute-done.19.refs_9_), channel_id=1, source_target_pairs={{0,2},{1,3},{2,0},{3,1},{4,6},{5,7},{6,4},{7,5},{8,10},{9,11},{10,... | collective-permute-start | bytes 1572872 | tf_op jit(solution)/shard_map/ppermute | solution.py:345
  57.3 10.0 %collective-permute-start.8 = (bf16[2,256,128]{2,1,0:T(8,128)(2,1)}, bf16[2,256,128]{2,1,0:T(8,128)(2,1)}, u32[]{:S(2)}, u32[]{:S(2)}) collective-permute-start(bf16[2,256,128]{2,1,0:T(8,128)(2,1)} %get-tuple-element.51), channel_id=1, source_target_pairs={{0,32},{1,33},{2,34},{3,35},{4,36},{5,37},{6,38},{7,39},{8,40},{9,... | collective-permute-start | bytes 393224 | tf_op jit(solution)/shard_map/ppermute | solution.py:345
  58.2 13.5 %collective-permute-start.9 = (bf16[2,256,128]{2,1,0:T(8,128)(2,1)}, bf16[2,256,128]{2,1,0:T(8,128)(2,1)}, u32[]{:S(2)}, u32[]{:S(2)}) collective-permute-start(bf16[2,256,128]{2,1,0:T(8,128)(2,1)} %get-tuple-element.50.refs_0_), channel_id=1, source_target_pairs={{0,1},{1,0},{2,3},{3,2},{4,5},{5,4},{6,7},{7,6},{8,9},{9,8},{10,11... | collective-permute-start | bytes 393224 | tf_op jit(solution)/shard_map/ppermute | solution.py:345
  59.8 14.3 %collective-permute-start.10 = (bf16[2,256,128]{2,1,0:T(8,128)(2,1)}, bf16[2,256,128]{2,1,0:T(8,128)(2,1)}, u32[]{:S(2)}, u32[]{:S(2)}) collective-permute-start(bf16[2,256,128]{2,1,0:T(8,128)(2,1)} %get-tuple-element.51), channel_id=1, source_target_pairs={{0,33},{1,32},{2,35},{3,34},{4,37},{5,36},{6,39},{7,38},{8,41},{9,... | collective-permute-start | bytes 393224 | tf_op jit(solution)/shard_map/ppermute | solution.py:345
  66.3 12.6 %copy-start = (bf16[2,256,128]{2,1,0:T(8,128)(2,1)S(1)}, bf16[2,256,128]{2,1,0:T(8,128)(2,1)}, u32[]{:S(2)}) copy-start(bf16[2,256,128]{2,1,0:T(8,128)(2,1)} %get-tuple-element.50.refs_0_) | copy-start | bytes 393220
  66.3 12.6 %copy-start.1 = (bf16[2,256,128]{2,1,0:T(8,128)(2,1)S(1)}, bf16[2,256,128]{2,1,0:T(8,128)(2,1)}, u32[]{:S(2)}) copy-start(bf16[2,256,128]{2,1,0:T(8,128)(2,1)} %get-tuple-element.54.refs_4_) | copy-start | bytes 393220
  66.3 7.8 %collective-permute-start.16 = (bf16[2,256,128]{2,1,0:T(8,128)(2,1)}, bf16[2,256,128]{2,1,0:T(8,128)(2,1)S(1)}, u32[]{:S(2)}, u32[]{:S(2)}) collective-permute-start(bf16[2,256,128]{2,1,0:T(8,128)(2,1)} %get-tuple-element.55), channel_id=1, source_target_pairs={{0,32},{1,33},{2,34},{3,35},{4,36},{5,37},{6,38},{7,39},{8,40},{9,... | collective-permute-start | bytes 393224 | tf_op jit(solution)/shard_map/ppermute | solution.py:345
  67.3 11.5 %collective-permute-start.18 = (bf16[2,256,128]{2,1,0:T(8,128)(2,1)}, bf16[2,256,128]{2,1,0:T(8,128)(2,1)S(1)}, u32[]{:S(2)}, u32[]{:S(2)}) collective-permute-start(bf16[2,256,128]{2,1,0:T(8,128)(2,1)} %get-tuple-element.55), channel_id=1, source_target_pairs={{0,33},{1,32},{2,35},{3,34},{4,37},{5,36},{6,39},{7,38},{8,41},{9,... | collective-permute-start | bytes 393224 | tf_op jit(solution)/shard_map/ppermute | solution.py:345
  71.7 7.2 %collective-permute-start.17 = (bf16[2,256,128]{2,1,0:T(8,128)(2,1)}, bf16[2,256,128]{2,1,0:T(8,128)(2,1)S(1)}, u32[]{:S(2)}, u32[]{:S(2)}) collective-permute-start(bf16[2,256,128]{2,1,0:T(8,128)(2,1)} %get-tuple-element.54.refs_4_), channel_id=1, source_target_pairs={{0,1},{1,0},{2,3},{3,2},{4,5},{5,4},{6,7},{7,6},{8,9},{9,8},{10,11... | collective-permute-start | bytes 393224 | tf_op jit(solution)/shard_map/ppermute | solution.py:345
where the time goes:
time: 84.3 us; the launch traced here: 83.5 us
  starting transfers between devices  33.3 us (40%)
  Pallas kernels  31.9 us (38%)
  waiting for transfers between devices  11.2 us (13%)
  local copies, waits for them, and re-layouts  6.78 us (8%)
    ppermute x21, starting transfers between devices, moved(): return lambda shard: lax.ppermute(shard, AXES, pairs)  33.3 us
    pallas_call x2, Pallas kernels, attend(): pl.pallas_call(functools.partial(attend_kernel, head), out_shape=[bf16(2,...  13.8 us
    ppermute x21, waiting for transfers between devices, moved(): return lambda shard: lax.ppermute(shard, AXES, pairs)  11.2 us
    pallas_call x2, Pallas kernels, project(): pl.pallas_call(functools.partial(project_kernel, blocks, chunks), out_sha...  9.41 us
    pallas_call x1, Pallas kernels, mix(): pl.pallas_call(mix_kernel, out_shape=bf16(rows, width), in_specs=[ANY] *...  4.42 us
    pallas_call x2, Pallas kernels, gather(): pl.pallas_call(gather_kernel, out_shape=[bf16(2, 4, TILE, HD), bf16(2, 3,...  4.22 us
    dynamic_slice x3, local copies, waits for them, and re-layouts, cached(): lax.dynamic_slice_in_dim(context_kv, (PAIR * x_lo + head) * HD, HD, 4)  3.6 us
    dynamic_slice x1, local copies, waits for them, and re-layouts, fetched(): lax.dynamic_slice(w_out, (core * PAIR * HD, (1 - x_hi) * half), (PAIR * H...  1.88 us
  transfers between devices with their start and end apart: 21, of which 3 were waited for; matrix products, arithmetic and copies ran while one was open for 8% of the time, Pallas kernels for 26%

commit v1 on v0

--- a/solution.py
+++ b/solution.py
@@ -18,15 +18,7 @@
 VMEM = pl.BlockSpec(memory_space=pltpu.VMEM)
 SMEM = pl.BlockSpec(memory_space=pltpu.SMEM)
 PARAMS = pltpu.CompilerParams(vmem_limit_bytes=64 * MIB)
-SMALL = pl.CostEstimate(flops=1000, bytes_accessed=1000, transcendentals=0)
-
-
-def cost(us):
-    return pl.CostEstimate(flops=int(us * 1.15e9), bytes_accessed=1000, transcendentals=0)
-
-
-C_SEND, C_OWN, C_GATHER, C_ATTEND, C_MIX = 1, 1, 2, 1, 1
-SPLIT, CTX_FIRST, Q_AFTER, OUTER_B, W_AFTER, EXCH = 0, 1, 2, 1, 1, 0
+SMALL = pl.CostEstimate(flops=10**9, bytes_accessed=1000, transcendentals=0)
 
 
 def pairs_of(sizes, move):
@@ -86,7 +78,7 @@
                 outs[out][head] = piece
 
 
-def project(blocks, shapes, tokens, w3, estimate):
+def project(blocks, shapes, tokens, w3):
     rows, width = tokens.shape
     chunks = 4
     return pl.pallas_call(
@@ -101,7 +93,7 @@
             pltpu.SemaphoreType.DMA((chunks, len(blocks))),
         ],
         compiler_params=PARAMS,
-        cost_estimate=estimate,
+        cost_estimate=SMALL,
     )(tokens, w3)
 
 
@@ -139,7 +131,7 @@
         out_specs=[VMEM] * 2,
         scratch_shapes=[pltpu.SemaphoreType.DMA((4,))],
         compiler_params=PARAMS,
-        cost_estimate=cost(C_GATHER),
+        cost_estimate=SMALL,
     )(kvx, kvm, ctx)
 
 
@@ -268,69 +260,73 @@
             pltpu.SemaphoreType.DMA((14,)),
         ],
         compiler_params=PARAMS,
-        cost_estimate=cost(C_ATTEND),
+        cost_estimate=SMALL,
     )(windows, edges, q_own, q_far, *pieces)
 
 
 def mix_kernel(*refs):
-    pieces, (w_own, w_mine, w_core, out, held, w, made, sem_a, sem_o) = refs[:8], refs[8:]
-    mine, core = x_low(), lax.axis_index("cam") % 2
+    pieces, (w_out, w_mine, w_core, out, first, second, w, made, sem_a, sem_w, sem_o) = refs[:8], refs[8:]
+    mine, core, head = x_low(), lax.axis_index("cam") % 2, lax.axis_index("head")
     part = PAIR * HD
-    width = w_own.shape[1]
+    width = w.shape[1]
     half = width // 2
     rows = lambda at: pl.ds(pl.multiple_of(at, part), part)
-    inputs = started(
-        [(piece, held.at[n % 4, :, :, pl.ds(n // 4 * HD, HD)]) for n, piece in enumerate(pieces)],
-        [sem_a.at[i] for i in range(8)],
-    )
-
-    @pl.when(core == mine)
-    def _():
-        w[0], w[1] = w_mine[...], w_core[...]
-
-    @pl.when(core != mine)
-    def _():
-        w[0], w[1] = w_core[...], w_mine[...]
-
+    pairs = []
+    for n, piece in enumerate(pieces):
+        held = (first, second)[n // 4]
+        pairs.append((piece, held.at[:, :, pl.ds(n % 4 * HD, HD)]))
+    inputs = started(pairs, [sem_a.at[i] for i in range(8)])
+    weights = []
+    for n in range(2):
+        cols = pl.ds(n * half, half)
+        there = pl.ds(pl.multiple_of(head * width + n * half, half), half)
+        pairs = [
+            (w_out.at[rows(part * mine), there], w.at[pl.ds(0, part), cols]),
+            (w_out.at[rows(part * (1 - mine)), there], w.at[pl.ds(part, part), cols]),
+            (w_mine.at[:, cols], w.at[rows(jnp.where(core == mine, 2, 3) * part), cols]),
+            (w_core.at[:, cols], w.at[rows(jnp.where(core == mine, 3, 2) * part), cols]),
+        ]
+        weights.append(started(pairs, [sem_w.at[n, i] for i in range(4)]))
     for copy in inputs:
         copy.wait()
 
-    def group(first, weights, cols):
-        total = None
-        for n, weight in enumerate(weights):
-            both = held[first + n].reshape(2 * TILE, part)
-            term = jnp.dot(both, weight[:, cols], preferred_element_type=jnp.float32)
-            total = term if total is None else total + term
+    def group(held, at, cols):
+        total = jnp.dot(
+            held[...].reshape(2 * TILE, 2 * part), w[at : at + 2 * part, cols], preferred_element_type=jnp.float32
+        )
         return total.astype(jnp.bfloat16).astype(jnp.float32)
 
     outs = []
     for n in range(2):
+        for copy in weights[n]:
+            copy.wait()
         cols = slice(n * half, (n + 1) * half)
-        first = group(0, (w_own.at[rows(part * mine)], w_own.at[rows(part * (1 - mine))]), cols)
-        second = group(2, (w.at[0], w.at[1]), cols)
-        made[n] = (first + second).astype(jnp.bfloat16)
+        made[n] = (group(first, 0, cols) + group(second, 2 * part, cols)).astype(jnp.bfloat16)
         outs += started([(made.at[n], out.at[:, pl.ds(n * half, half)])], [sem_o.at[n]])
     for copy in outs:
         copy.wait()
 
 
-def mix(attended, w_own, w_mine, w_core):
-    rows, width = 2 * TILE, w_own.shape[1]
+def mix(attended, w_out, w_mine, w_core):
+    rows = 2 * TILE
+    width = w_out.shape[1] // 2
     return pl.pallas_call(
         mix_kernel,
         out_shape=bf16(rows, width),
-        in_specs=[ANY] * 8 + [VMEM] * 3,
+        in_specs=[ANY] * 11,
         out_specs=ANY,
         scratch_shapes=[
-            pltpu.VMEM((4, 2, TILE, PAIR * HD), jnp.bfloat16),
-            pltpu.VMEM((2,) + w_mine.shape, jnp.bfloat16),
+            pltpu.VMEM((2, TILE, 2 * PAIR * HD), jnp.bfloat16),
+            pltpu.VMEM((2, TILE, 2 * PAIR * HD), jnp.bfloat16),
+            pltpu.VMEM((4 * PAIR * HD, width), jnp.bfloat16),
             pltpu.VMEM((2, rows, width // 2), jnp.bfloat16),
             pltpu.SemaphoreType.DMA((8,)),
+            pltpu.SemaphoreType.DMA((2, 4)),
             pltpu.SemaphoreType.DMA((2,)),
         ],
-        compiler_params=pltpu.CompilerParams(vmem_limit_bytes=24 * MIB),
-        cost_estimate=cost(C_MIX),
-    )(*attended, w_own, w_mine, w_core)
+        compiler_params=PARAMS,
+        cost_estimate=SMALL,
+    )(*attended, w_out, w_mine, w_core)
 
 
 def body(tokens, w_qkv, w_out, window_len, edge_counts, context_kv):
@@ -358,84 +354,44 @@
     kv_shape = bf16(1, 2, frames, TILE, HD)
     q_shape = bf16(PAIR, frames, TILE, HD)
 
-    sent = project([(1, False, 0, (0,)), (2, False, 0, (1,))], [kv_shape] * 2, flat, w3, cost(C_SEND))
-    kvx = [to_mate(one[0]) for one in sent]
-    if not SPLIT:
-        kvx = lax.optimization_barrier(kvx)
-
-    def cached(context_kv):
-        ctx = []
-        for head in range(PAIR):
-            part = lax.dynamic_slice_in_dim(context_kv, (PAIR * x_lo + head) * HD, HD, 4)
-            ctx.append(jnp.transpose(part.reshape(WMAX - 1, TILE, 2, HD), (2, 0, 1, 3)))
-        return ctx
-
-    if CTX_FIRST:
-        ctx = cached(lax.optimization_barrier((context_kv, sent))[0])
-        flat, _ = lax.optimization_barrier((flat, ctx))
-    else:
-        flat, _ = lax.optimization_barrier((flat, sent))
+    sent = project([(1, False, 0, (0,)), (2, False, 0, (1,))], [kv_shape] * 2, flat, w3)
+    hold = lambda x, *after: lax.optimization_barrier((x, after))[0]
+    kvx = [to_mate(sent[0][0])]
     *kvm, q_sent, q_own = project(
         [(1, True, 0, (0,)), (2, True, 0, (1,)), (0, False, 2, ()), (0, True, 3, ())],
         [kv_shape] * 2 + [q_shape] * 2,
-        flat,
+        hold(flat, sent),
         w3,
-        cost(C_OWN),
     )
-    if not CTX_FIRST:
-        ctx = cached(lax.optimization_barrier((context_kv, q_own))[0])
-    if Q_AFTER:
-        q_sent, _ = lax.optimization_barrier((q_sent, kvx[Q_AFTER - 1]))
-    q_far = to_mate(q_sent)
-
-    four, halo = [], []
+    kvx.append(to_mate(hold(sent[1], q_own)[0]))
+    q_far = to_mate(hold(q_sent, kvx[1]))
+
+    four, later = [], []
     for head in range(PAIR):
-        one, later = gather(kvx[head], kvm[head][0], ctx[head])
-        outer = one
-        if head and OUTER_B == 1:
-            outer, q_far, four[0] = lax.optimization_barrier((one, q_far, four[0]))
-        if head and OUTER_B == 2:
-            outer, halo[0] = lax.optimization_barrier((one, halo[0]))
+        ctx = lax.dynamic_slice_in_dim(hold(context_kv, q_own), (PAIR * x_lo + head) * HD, HD, 4)
+        ctx = jnp.transpose(ctx.reshape(WMAX - 1, TILE, 2, HD), (2, 0, 1, 3))
+        one, halo = gather(kvx[head], kvm[head][0], ctx)
+        later.append(to_later(halo))
+        outer = hold(one, four[0], q_far) if head else one
         four.append([one, to_right(outer), to_left(outer)])
-        halo.append(to_later(later))
-        if head == 0 or OUTER_B != 3:
-            halo[head] = wide(halo[head])
-        else:
-            later, four = lax.optimization_barrier((halo[1], four))
-            halo[1] = wide(later)
+    halo = [wide(one) for one in later]
 
     half = w_out.shape[1] // 2
-
-    def fetched(w_out):
-        w_part = lax.dynamic_slice(w_out, (core * PAIR * HD, (1 - x_hi) * half), (PAIR * HD, half))
-        return to_diag(w_part)
-
-    if W_AFTER == 0:
-        w_mine = fetched(w_out)
-    if W_AFTER == 1:
-        w_mine = fetched(lax.optimization_barrier((w_out, four[1][0]))[0])
-    if W_AFTER == 2:
-        w_now, four[1] = lax.optimization_barrier((w_out, four[1]))
-        w_mine = fetched(w_now)
-    if W_AFTER == 3:
-        w_now, halo[0] = lax.optimization_barrier((w_out, halo[0]))
-        w_mine = fetched(w_now)
+    w_part = lax.dynamic_slice(
+        hold(w_out, four[0][0]), (core * PAIR * HD, (1 - x_hi) * half), (PAIR * HD, half)
+    )
+    w_mine = to_diag(w_part)
 
     pieces = []
     for head in range(PAIR):
-        own, mates = attend(head, window_len, edge_counts, q_own, q_far, four[head] + halo[head])
-        if head:
-            if EXCH:
-                own, mates, pieces = lax.optimization_barrier((own, mates, pieces))
+        mine, mates = attend(head, window_len, edge_counts, q_own, q_far, four[head] + halo[head])
+        if head == 0:
+            w_core = to_core(hold(w_mine, mine))
         else:
-            if W_AFTER == 4:
-                w_mine = fetched(lax.optimization_barrier((w_out, own))[0])
-            else:
-                w_mine, _ = lax.optimization_barrier((w_mine, own))
-            w_core = to_core(w_mine)
-            w_own = lax.dynamic_slice_in_dim(lax.optimization_barrier((w_out, own))[0], x_hi * half, half, 1)
-        pieces.append([own, to_mate(mates), to_over(own), to_diag(mates)])
-    out = mix(pieces[0] + pieces[1], w_own, w_mine, w_core)
+            mine, mates, pieces = lax.optimization_barrier((mine, mates, pieces))
+        pieces.append([mine, to_mate(mates), to_over(mine), to_diag(mates)])
+    attended = [piece for both in zip(*pieces) for piece in both]
+    out = mix(attended, w_out, w_mine, w_core)
     return out.reshape(frames, cols, row_count, -1)
 
 

time: 84.3 us -> 83.3 us (0.988)
  starting transfers between devices: 33.3 us -> 29.8 us
  waiting for transfers between devices: 11.2 us -> 13.7 us
    ppermute x21, starting transfers between devices: 33.3 us -> 29.8 us  [moved(): return lambda shard: lax.ppermute(shard, AXES, pairs)]
    ppermute x21, waiting for transfers between devices: 11.2 us -> 13.7 us  [moved(): return lambda shard: lax.ppermute(shard, AXES, pairs)]
    dynamic_slice x5 -> x4, local copies, waits for them, and re-layouts: 6.77 us -> 7.17 us  [the longest x3 5.3 us: body(): lax.dynamic_slice_in_dim(hold(context_kv, q_own), (PAIR * x_lo + head) *...]
  transfers between devices with their start and end apart: 21 -> 21, of which waited for: 3 -> 6; matrix products, arithmetic and copies ran while one was open for 8% -> 9% of each run, Pallas kernels for 26% -> 29%
where the time goes in v1:
time: 83.3 us; the launch traced here: 82.6 us
  Pallas kernels  31.7 us (38%)
  starting transfers between devices  29.8 us (36%)
  waiting for transfers between devices  13.7 us (16%)
  local copies, waits for them, and re-layouts  7.17 us (9%)
    ppermute x21, starting transfers between devices, moved(): return lambda shard: lax.ppermute(shard, AXES, pairs)  29.8 us
    pallas_call x2, Pallas kernels, attend(): pl.pallas_call(functools.partial(attend_kernel, head), out_shape=[bf16(2,...  13.8 us
    ppermute x21, waiting for transfers between devices, moved(): return lambda shard: lax.ppermute(shard, AXES, pairs)  13.7 us
    pallas_call x2, Pallas kernels, project(): pl.pallas_call(functools.partial(project_kernel, blocks, chunks), out_sha...  9.42 us
    dynamic_slice x3, local copies, waits for them, and re-layouts, body(): lax.dynamic_slice_in_dim(hold(context_kv, q_own), (PAIR * x_lo + head) *...  5.3 us
    pallas_call x1, Pallas kernels, mix(): pl.pallas_call(mix_kernel, out_shape=bf16(rows, width), in_specs=[ANY] *...  4.27 us
    pallas_call x2, Pallas kernels, gather(): pl.pallas_call(gather_kernel, out_shape=[bf16(2, 4, TILE, HD), bf16(2, 3,...  4.22 us
    dynamic_slice x1, local copies, waits for them, and re-layouts, body(): lax.dynamic_slice(hold(w_out, four[0][0]), (core * PAIR * HD, (1 - x_hi)...  1.87 us
  transfers between devices with their start and end apart: 21, of which 6 were waited for; matrix products, arithmetic and copies ran while one was open for 9% of the time, Pallas kernels for 29%

profile of v1, /device:TPU:1, one launch (start us, length us, event | category | flops | bytes accessed | tf_op | source)
XLA Modules:
  0.0 82.6 jit_solution(16251985355589872857)
XLA Ops:
  0.0 3.8 %shard_map.64 = (bf16[1,2,2,256,128]{4,3,2,1,0:T(8,128)(2,1)}, bf16[1,2,2,256,128]{4,3,2,1,0:T(8,128)(2,1)}) custom-call(bf16[512,2048]{1,0:T(8,128)(2,1)} %bitcast.15, bf16[3,2048,512]{2,1,0:T(8,128)(2,1)} %bitcast.13), custom_call_target="tpu_custom_call" | custom-call | flops 1000000000 | bytes 1000 | tf_op jit(solution)/shard_map/pallas_call | solution.py:84
  3.8 2.1 %collective-permute-start.2 = (bf16[2,2,256,128]{3,2,1,0:T(8,128)(2,1)}, bf16[2,2,256,128]{3,2,1,0:T(8,128)(2,1)}, u32[]{:S(2)}, u32[]{:S(2)}) collective-permute-start(bf16[2,2,256,128]{3,2,1,0:T(8,128)(2,1)} %bitcast.22), channel_id=1, source_target_pairs={{0,32},{1,33},{2,34},{3,35},{4,36},{5,37},{6,38},{7,39},{8,40},{9,... | collective-permute-start | bytes 786440 | tf_op jit(solution)/shard_map/ppermute | solution.py:341
  5.9 5.7 %shard_map.65 = (bf16[1,2,2,256,128]{4,3,2,1,0:T(8,128)(2,1)}, bf16[1,2,2,256,128]{4,3,2,1,0:T(8,128)(2,1)}, bf16[2,2,256,128]{3,2,1,0:T(8,128)(2,1)}, bf16[2,2,256,128]{3,2,1,0:T(8,128)(2,1)}) custom-call(bf16[512,2048]{1,0:T(8,128)(2,1)} %bitcast.16, bf16[3,2048,512]{2,1,0:T(8,128)(2,1)} %bitcast.14), custom_call_target="tpu_custom_call" | custom-call | flops 1000000000 | bytes 1000 | tf_op jit(solution)/shard_map/pallas_call | solution.py:84
  11.7 2.7 %constant_dynamic-slice_fusion = (bf16[3,8,32,2,128]{4,3,2,1,0:T(2,128)(2,1)S(1)}, bf16[3,8,32,2,128]{4,3,2,1,0:T(2,128)(2,1)}) fusion(bf16[3,8,32,2,512]{4,3,2,1,0:T(2,128)(2,1)} %param.11, s32[]{:T(128)S(6)} %select_n.25, s32[]{:T(128)S(6)} %select_n.24), kind=kLoop, calls=%fused_computation | loop fusion | bytes 1572872 | tf_op jit(solution)/shard_map/dynamic_slice | solution.py:371
  15.2 2.1 %shard_map.67 = (bf16[2,4,256,128]{3,2,1,0:T(8,128)(2,1)}, bf16[2,3,256,128]{3,2,1,0:T(8,128)(2,1)}) custom-call(bf16[2,2,256,128]{3,2,1,0:T(8,128)(2,1)} %collective-permute-done.2.kvx, bf16[2,2,256,128]{3,2,1,0:T(8,128)(2,1)} %bitcast.21, bf16[2,3,256,128]{3,2,1,0:T(8,128)(2,1)} %bitcast.17), custom_call_target="tpu_custom_call" | custom-call | flops 1000000000 | bytes 1000 | tf_op jit(solution)/shard_map/pallas_call | solution.py:127
  17.3 3.0 %collective-permute-start.3 = (bf16[2,4,256,128]{3,2,1,0:T(8,128)(2,1)}, bf16[2,4,256,128]{3,2,1,0:T(8,128)(2,1)}, u32[]{:S(2)}, u32[]{:S(2)}) collective-permute-start(bf16[2,4,256,128]{3,2,1,0:T(8,128)(2,1)} %get-tuple-element.43.refs_0_), channel_id=1, source_target_pairs={{0,2},{1,3},{2,4},{3,5},{4,6},{5,7},{6,8},{7,9},{8,10},{9,11},{10,... | collective-permute-start | bytes 1572872 | tf_op jit(solution)/shard_map/ppermute | solution.py:341
  20.3 1.3 %collective-permute-start.10 = (bf16[2,3,256,128]{3,2,1,0:T(8,128)(2,1)}, bf16[2,3,256,128]{3,2,1,0:T(8,128)(2,1)}, u32[]{:S(2)}, u32[]{:S(2)}) collective-permute-start(bf16[2,3,256,128]{3,2,1,0:T(8,128)(2,1)} %get-tuple-element.48), channel_id=1, source_target_pairs={{0,64},{1,65},{2,66},{3,67},{4,68},{5,69},{6,70},{7,71},{8,72},{9,... | collective-permute-start | bytes 1179656 | tf_op jit(solution)/shard_map/ppermute | solution.py:341
  22.8 1.8 %copy.7 = bf16[3,8,32,2,128]{4,2,1,0,3:T(8,128)(2,1)} copy(bf16[3,8,32,2,128]{4,3,2,1,0:T(2,128)(2,1)} %get-tuple-element.60) | data formatting | bytes 786432 | tf_op jit(solution)/shard_map/dynamic_slice | solution.py:371
  24.6 2.1 %shard_map.66 = (bf16[2,4,256,128]{3,2,1,0:T(8,128)(2,1)}, bf16[2,3,256,128]{3,2,1,0:T(8,128)(2,1)}) custom-call(bf16[2,2,256,128]{3,2,1,0:T(8,128)(2,1)} %collective-permute-done.kvx, bf16[2,2,256,128]{3,2,1,0:T(8,128)(2,1)} %bitcast.19, bf16[2,3,256,128]{3,2,1,0:T(8,128)(2,1)} %bitcast.18), custom_call_target="tpu_custom_call" | custom-call | flops 1000000000 | bytes 1000 | tf_op jit(solution)/shard_map/pallas_call | solution.py:127
  26.7 1.4 %collective-permute-start.7 = (bf16[2,3,256,128]{3,2,1,0:T(8,128)(2,1)}, bf16[2,3,256,128]{3,2,1,0:T(8,128)(2,1)}, u32[]{:S(2)}, u32[]{:S(2)}) collective-permute-start(bf16[2,3,256,128]{3,2,1,0:T(8,128)(2,1)} %get-tuple-element.45), channel_id=1, source_target_pairs={{0,64},{1,65},{2,66},{3,67},{4,68},{5,69},{6,70},{7,71},{8,72},{9,... | collective-permute-start | bytes 1179656 | tf_op jit(solution)/shard_map/ppermute | solution.py:341
  28.1 4.3 %collective-permute-done.10.refs_3_ = bf16[2,3,256,128]{3,2,1,0:T(8,128)(2,1)} collective-permute-done((bf16[2,3,256,128]{3,2,1,0:T(8,128)(2,1)}, bf16[2,3,256,128]{3,2,1,0:T(8,128)(2,1)}, u32[]{:S(2)}, u32[]{:S(2)}) %collective-permute-start.10) | collective-permute-done | bytes 393248 | tf_op jit(solution)/shard_map/ppermute | solution.py:341
  34.1 1.9 %dynamic_slice.11 = bf16[256,1024]{1,0:T(8,128)(2,1)} dynamic-slice(bf16[512,2048]{1,0:T(8,128)(2,1)} %refs_8_.1, s32[]{:T(128)S(6)} %select_n.27, s32[]{:T(128)S(6)} %select_n.28), dynamic_slice_sizes={256,1024} | dynamic-slice | bytes 1048580 | tf_op jit(solution)/shard_map/dynamic_slice | solution.py:380
  37.2 2.3 %collective-permute-start.5 = (bf16[2,4,256,128]{3,2,1,0:T(8,128)(2,1)}, bf16[2,4,256,128]{3,2,1,0:T(8,128)(2,1)}, u32[]{:S(2)}, u32[]{:S(2)}) collective-permute-start(bf16[2,4,256,128]{3,2,1,0:T(8,128)(2,1)} %get-tuple-element.44.refs_0_), channel_id=1, source_target_pairs={{0,2},{1,3},{2,4},{3,5},{4,6},{5,7},{6,8},{7,9},{8,10},{9,11},{10,... | collective-permute-start | bytes 1572872 | tf_op jit(solution)/shard_map/ppermute | solution.py:341
  39.6 2.2 %collective-permute-start.6 = (bf16[2,4,256,128]{3,2,1,0:T(8,128)(2,1)}, bf16[2,4,256,128]{3,2,1,0:T(8,128)(2,1)}, u32[]{:S(2)}, u32[]{:S(2)}) collective-permute-start(bf16[2,4,256,128]{3,2,1,0:T(8,128)(2,1)} %get-tuple-element.44.refs_0_), channel_id=1, source_target_pairs={{0,30},{1,31},{2,0},{3,1},{4,2},{5,3},{6,4},{7,5},{8,6},{9,7},{10,... | collective-permute-start | bytes 1572872 | tf_op jit(solution)/shard_map/ppermute | solution.py:341
  43.3 8.8 %shard_map.69 = (bf16[2,256,128]{2,1,0:T(8,128)(2,1)}, bf16[2,256,128]{2,1,0:T(8,128)(2,1)}) custom-call(s32[4]{0:T(128)} %windows.3, s32[16]{0:T(128)} %edges.3, bf16[2,2,256,128]{3,2,1,0:T(8,128)(2,1)} %get-tuple-element.35.q_own, bf16[2,2,256,128]{3,2,1,0:T(8,128)(2,1)} %collective-permute-done.1.q_far, ...), custom_call_target="tpu_custom_call" | custom-call | flops 1000000000 | bytes 1000 | tf_op jit(solution)/shard_map/pallas_call | solution.py:243
  52.1 3.0 %collective-permute-start.20 = (bf16[256,1024]{1,0:T(8,128)(2,1)}, bf16[256,1024]{1,0:T(8,128)(2,1)}, u32[]{:S(2)}, u32[]{:S(2)}) collective-permute-start(bf16[256,1024]{1,0:T(8,128)(2,1)} %collective-permute-done.19.refs_9_), channel_id=1, source_target_pairs={{0,2},{1,3},{2,0},{3,1},{4,6},{5,7},{6,4},{7,5},{8,10},{9,11},{10,... | collective-permute-start | bytes 1572872 | tf_op jit(solution)/shard_map/ppermute | solution.py:341
  56.3 2.2 %collective-permute-start.15 = (bf16[2,256,128]{2,1,0:T(8,128)(2,1)}, bf16[2,256,128]{2,1,0:T(8,128)(2,1)}, u32[]{:S(2)}, u32[]{:S(2)}) collective-permute-start(bf16[2,256,128]{2,1,0:T(8,128)(2,1)} %get-tuple-element.50), channel_id=1, source_target_pairs={{0,33},{1,32},{2,35},{3,34},{4,37},{5,36},{6,39},{7,38},{8,41},{9,... | collective-permute-start | bytes 393224 | tf_op jit(solution)/shard_map/ppermute | solution.py:341
  58.4 5.0 %shard_map.68 = (bf16[2,256,128]{2,1,0:T(8,128)(2,1)}, bf16[2,256,128]{2,1,0:T(8,128)(2,1)}) custom-call(s32[4]{0:T(128)} %windows.3, s32[16]{0:T(128)} %edges.3, bf16[2,2,256,128]{3,2,1,0:T(8,128)(2,1)} %get-tuple-element.35.q_own, bf16[2,2,256,128]{3,2,1,0:T(8,128)(2,1)} %collective-permute-done.1.q_far, ...), custom_call_target="tpu_custom_call" | custom-call | flops 1000000000 | bytes 1000 | tf_op jit(solution)/shard_map/pallas_call | solution.py:243
  63.5 1.7 %collective-permute-done.15.refs_6_ = bf16[2,256,128]{2,1,0:T(8,128)(2,1)} collective-permute-done((bf16[2,256,128]{2,1,0:T(8,128)(2,1)}, bf16[2,256,128]{2,1,0:T(8,128)(2,1)}, u32[]{:S(2)}, u32[]{:S(2)}) %collective-permute-start.15) | collective-permute-done | bytes 131104 | tf_op jit(solution)/shard_map/ppermute | solution.py:341
  65.2 2.9 %collective-permute-start.16 = (bf16[2,256,128]{2,1,0:T(8,128)(2,1)}, bf16[2,256,128]{2,1,0:T(8,128)(2,1)}, u32[]{:S(2)}, u32[]{:S(2)}) collective-permute-start(bf16[2,256,128]{2,1,0:T(8,128)(2,1)} %get-tuple-element.54), channel_id=1, source_target_pairs={{0,32},{1,33},{2,34},{3,35},{4,36},{5,37},{6,38},{7,39},{8,40},{9,... | collective-permute-start | bytes 393224 | tf_op jit(solution)/shard_map/ppermute | solution.py:341
  68.5 2.1 %collective-permute-start.18 = (bf16[2,256,128]{2,1,0:T(8,128)(2,1)}, bf16[2,256,128]{2,1,0:T(8,128)(2,1)}, u32[]{:S(2)}, u32[]{:S(2)}) collective-permute-start(bf16[2,256,128]{2,1,0:T(8,128)(2,1)} %get-tuple-element.54), channel_id=1, source_target_pairs={{0,33},{1,32},{2,35},{3,34},{4,37},{5,36},{6,39},{7,38},{8,41},{9,... | collective-permute-start | bytes 393224 | tf_op jit(solution)/shard_map/ppermute | solution.py:341
  71.3 2.7 %collective-permute-done.17.refs_5_ = bf16[2,256,128]{2,1,0:T(8,128)(2,1)} collective-permute-done((bf16[2,256,128]{2,1,0:T(8,128)(2,1)}, bf16[2,256,128]{2,1,0:T(8,128)(2,1)}, u32[]{:S(2)}, u32[]{:S(2)}) %collective-permute-start.17) | collective-permute-done | bytes 131104 | tf_op jit(solution)/shard_map/ppermute | solution.py:341
  74.0 4.2 %collective-permute-done.18.refs_7_ = bf16[2,256,128]{2,1,0:T(8,128)(2,1)} collective-permute-done((bf16[2,256,128]{2,1,0:T(8,128)(2,1)}, bf16[2,256,128]{2,1,0:T(8,128)(2,1)}, u32[]{:S(2)}, u32[]{:S(2)}) %collective-permute-start.18) | collective-permute-done | bytes 131104 | tf_op jit(solution)/shard_map/ppermute | solution.py:341
  78.2 4.3 %shard_map.70 = bf16[512,1024]{1,0:T(8,128)(2,1)} custom-call(bf16[2,256,128]{2,1,0:T(8,128)(2,1)} %get-tuple-element.51.refs_0_, bf16[2,256,128]{2,1,0:T(8,128)(2,1)} %get-tuple-element.52.refs_1_, bf16[2,256,128]{2,1,0:T(8,128)(2,1)} %collective-permute-done.13.refs_2_, bf16[2,256,128]{2,1,0:T(8,128)(2,1)} %collective-permute-done.16.refs_3_, ...), custom_call_target="tpu_custom_call" | custom-call | flops 1000000000 | bytes 1000 | tf_op jit(solution)/shard_map/pallas_call | solution.py:313
  (29 shorter events, 9.1 us)
Async XLA Ops:
  3.8 11.4 %collective-permute-start.2 = (bf16[2,2,256,128]{3,2,1,0:T(8,128)(2,1)}, bf16[2,2,256,128]{3,2,1,0:T(8,128)(2,1)}, u32[]{:S(2)}, u32[]{:S(2)}) collective-permute-start(bf16[2,2,256,128]{3,2,1,0:T(8,128)(2,1)} %bitcast.22), channel_id=1, source_target_pairs={{0,32},{1,33},{2,34},{3,35},{4,36},{5,37},{6,38},{7,39},{8,40},{9,... | collective-permute-start | bytes 786440 | tf_op jit(solution)/shard_map/ppermute | solution.py:341
  11.6 10.0 %collective-permute-start = (bf16[2,2,256,128]{3,2,1,0:T(8,128)(2,1)}, bf16[2,2,256,128]{3,2,1,0:T(8,128)(2,1)}, u32[]{:S(2)}, u32[]{:S(2)}) collective-permute-start(bf16[2,2,256,128]{3,2,1,0:T(8,128)(2,1)} %bitcast.20), channel_id=1, source_target_pairs={{0,32},{1,33},{2,34},{3,35},{4,36},{5,37},{6,38},{7,39},{8,40},{9,... | collective-permute-start | bytes 786440 | tf_op jit(solution)/shard_map/ppermute | solution.py:341
  17.3 18.6 %collective-permute-start.3 = (bf16[2,4,256,128]{3,2,1,0:T(8,128)(2,1)}, bf16[2,4,256,128]{3,2,1,0:T(8,128)(2,1)}, u32[]{:S(2)}, u32[]{:S(2)}) collective-permute-start(bf16[2,4,256,128]{3,2,1,0:T(8,128)(2,1)} %get-tuple-element.43.refs_0_), channel_id=1, source_target_pairs={{0,2},{1,3},{2,4},{3,5},{4,6},{5,7},{6,8},{7,9},{8,10},{9,11},{10,... | collective-permute-start | bytes 1572872 | tf_op jit(solution)/shard_map/ppermute | solution.py:341
  20.3 12.1 %collective-permute-start.10 = (bf16[2,3,256,128]{3,2,1,0:T(8,128)(2,1)}, bf16[2,3,256,128]{3,2,1,0:T(8,128)(2,1)}, u32[]{:S(2)}, u32[]{:S(2)}) collective-permute-start(bf16[2,3,256,128]{3,2,1,0:T(8,128)(2,1)} %get-tuple-element.48), channel_id=1, source_target_pairs={{0,64},{1,65},{2,66},{3,67},{4,68},{5,69},{6,70},{7,71},{8,72},{9,... | collective-permute-start | bytes 1179656 | tf_op jit(solution)/shard_map/ppermute | solution.py:341
  21.6 11.3 %collective-permute-start.1 = (bf16[2,2,256,128]{3,2,1,0:T(8,128)(2,1)}, bf16[2,2,256,128]{3,2,1,0:T(8,128)(2,1)}, u32[]{:S(2)}, u32[]{:S(2)}) collective-permute-start(bf16[2,2,256,128]{3,2,1,0:T(8,128)(2,1)} %get-tuple-element.38), channel_id=1, source_target_pairs={{0,32},{1,33},{2,34},{3,35},{4,36},{5,37},{6,38},{7,39},{8,40},{9,... | collective-permute-start | bytes 786440 | tf_op jit(solution)/shard_map/ppermute | solution.py:341
  22.8 14.4 %collective-permute-start.4 = (bf16[2,4,256,128]{3,2,1,0:T(8,128)(2,1)}, bf16[2,4,256,128]{3,2,1,0:T(8,128)(2,1)}, u32[]{:S(2)}, u32[]{:S(2)}) collective-permute-start(bf16[2,4,256,128]{3,2,1,0:T(8,128)(2,1)} %get-tuple-element.43.refs_0_), channel_id=1, source_target_pairs={{0,30},{1,31},{2,0},{3,1},{4,2},{5,3},{6,4},{7,5},{8,6},{9,7},{10,... | collective-permute-start | bytes 1572872 | tf_op jit(solution)/shard_map/ppermute | solution.py:341
  26.7 12.9 %collective-permute-start.7 = (bf16[2,3,256,128]{3,2,1,0:T(8,128)(2,1)}, bf16[2,3,256,128]{3,2,1,0:T(8,128)(2,1)}, u32[]{:S(2)}, u32[]{:S(2)}) collective-permute-start(bf16[2,3,256,128]{3,2,1,0:T(8,128)(2,1)} %get-tuple-element.45), channel_id=1, source_target_pairs={{0,64},{1,65},{2,66},{3,67},{4,68},{5,69},{6,70},{7,71},{8,72},{9,... | collective-permute-start | bytes 1179656 | tf_op jit(solution)/shard_map/ppermute | solution.py:341
  32.4 9.5 %collective-permute-start.11 = (bf16[2,3,256,128]{3,2,1,0:T(8,128)(2,1)}, bf16[2,3,256,128]{3,2,1,0:T(8,128)(2,1)}, u32[]{:S(2)}, u32[]{:S(2)}) collective-permute-start(bf16[2,3,256,128]{3,2,1,0:T(8,128)(2,1)} %collective-permute-done.10.refs_3_), channel_id=1, source_target_pairs={{0,2},{1,3},{2,4},{3,5},{4,6},{5,7},{6,8},{7,9},{8,10},{9,11},{10,... | collective-permute-start | bytes 1179656 | tf_op jit(solution)/shard_map/ppermute | solution.py:341
  32.9 9.3 %collective-permute-start.12 = (bf16[2,3,256,128]{3,2,1,0:T(8,128)(2,1)}, bf16[2,3,256,128]{3,2,1,0:T(8,128)(2,1)}, u32[]{:S(2)}, u32[]{:S(2)}) collective-permute-start(bf16[2,3,256,128]{3,2,1,0:T(8,128)(2,1)} %collective-permute-done.10.refs_3_), channel_id=1, source_target_pairs={{0,30},{1,31},{2,0},{3,1},{4,2},{5,3},{6,4},{7,5},{8,6},{9,7},{10,... | collective-permute-start | bytes 1179656 | tf_op jit(solution)/shard_map/ppermute | solution.py:341
  35.9 16.2 %collective-permute-start.19 = (bf16[256,1024]{1,0:T(8,128)(2,1)}, bf16[256,1024]{1,0:T(8,128)(2,1)}, u32[]{:S(2)}, u32[]{:S(2)}) collective-permute-start(bf16[256,1024]{1,0:T(8,128)(2,1)} %dynamic_slice.11), channel_id=1, source_target_pairs={{0,33},{1,32},{2,35},{3,34},{4,37},{5,36},{6,39},{7,38},{8,41},{9,... | collective-permute-start | bytes 1572872 | tf_op jit(solution)/shard_map/ppermute | solution.py:341
  37.2 19.1 %collective-permute-start.5 = (bf16[2,4,256,128]{3,2,1,0:T(8,128)(2,1)}, bf16[2,4,256,128]{3,2,1,0:T(8,128)(2,1)}, u32[]{:S(2)}, u32[]{:S(2)}) collective-permute-start(bf16[2,4,256,128]{3,2,1,0:T(8,128)(2,1)} %get-tuple-element.44.refs_0_), channel_id=1, source_target_pairs={{0,2},{1,3},{2,4},{3,5},{4,6},{5,7},{6,8},{7,9},{8,10},{9,11},{10,... | collective-permute-start | bytes 1572872 | tf_op jit(solution)/shard_map/ppermute | solution.py:341
  39.6 18.8 %collective-permute-start.6 = (bf16[2,4,256,128]{3,2,1,0:T(8,128)(2,1)}, bf16[2,4,256,128]{3,2,1,0:T(8,128)(2,1)}, u32[]{:S(2)}, u32[]{:S(2)}) collective-permute-start(bf16[2,4,256,128]{3,2,1,0:T(8,128)(2,1)} %get-tuple-element.44.refs_0_), channel_id=1, source_target_pairs={{0,30},{1,31},{2,0},{3,1},{4,2},{5,3},{6,4},{7,5},{8,6},{9,7},{10,... | collective-permute-start | bytes 1572872 | tf_op jit(solution)/shard_map/ppermute | solution.py:341
  41.8 13.3 %collective-permute-start.8 = (bf16[2,3,256,128]{3,2,1,0:T(8,128)(2,1)}, bf16[2,3,256,128]{3,2,1,0:T(8,128)(2,1)}, u32[]{:S(2)}, u32[]{:S(2)}) collective-permute-start(bf16[2,3,256,128]{3,2,1,0:T(8,128)(2,1)} %collective-permute-done.7.refs_3_), channel_id=1, source_target_pairs={{0,2},{1,3},{2,4},{3,5},{4,6},{5,7},{6,8},{7,9},{8,10},{9,11},{10,... | collective-permute-start | bytes 1179656 | tf_op jit(solution)/shard_map/ppermute | solution.py:341
  42.1 13.5 %collective-permute-start.9 = (bf16[2,3,256,128]{3,2,1,0:T(8,128)(2,1)}, bf16[2,3,256,128]{3,2,1,0:T(8,128)(2,1)}, u32[]{:S(2)}, u32[]{:S(2)}) collective-permute-start(bf16[2,3,256,128]{3,2,1,0:T(8,128)(2,1)} %collective-permute-done.7.refs_3_), channel_id=1, source_target_pairs={{0,30},{1,31},{2,0},{3,1},{4,2},{5,3},{6,4},{7,5},{8,6},{9,7},{10,... | collective-permute-start | bytes 1179656 | tf_op jit(solution)/shard_map/ppermute | solution.py:341
  52.1 26.0 %collective-permute-start.20 = (bf16[256,1024]{1,0:T(8,128)(2,1)}, bf16[256,1024]{1,0:T(8,128)(2,1)}, u32[]{:S(2)}, u32[]{:S(2)}) collective-permute-start(bf16[256,1024]{1,0:T(8,128)(2,1)} %collective-permute-done.19.refs_9_), channel_id=1, source_target_pairs={{0,2},{1,3},{2,0},{3,1},{4,6},{5,7},{6,4},{7,5},{8,10},{9,11},{10,... | collective-permute-start | bytes 1572872 | tf_op jit(solution)/shard_map/ppermute | solution.py:341
  55.2 8.4 %collective-permute-start.14 = (bf16[2,256,128]{2,1,0:T(8,128)(2,1)}, bf16[2,256,128]{2,1,0:T(8,128)(2,1)}, u32[]{:S(2)}, u32[]{:S(2)}) collective-permute-start(bf16[2,256,128]{2,1,0:T(8,128)(2,1)} %get-tuple-element.51.refs_0_), channel_id=1, source_target_pairs={{0,1},{1,0},{2,3},{3,2},{4,5},{5,4},{6,7},{7,6},{8,9},{9,8},{10,11... | collective-permute-start | bytes 393224 | tf_op jit(solution)/shard_map/ppermute | solution.py:341
  55.6 7.9 %collective-permute-start.13 = (bf16[2,256,128]{2,1,0:T(8,128)(2,1)}, bf16[2,256,128]{2,1,0:T(8,128)(2,1)}, u32[]{:S(2)}, u32[]{:S(2)}) collective-permute-start(bf16[2,256,128]{2,1,0:T(8,128)(2,1)} %get-tuple-element.50), channel_id=1, source_target_pairs={{0,32},{1,33},{2,34},{3,35},{4,36},{5,37},{6,38},{7,39},{8,40},{9,... | collective-permute-start | bytes 393224 | tf_op jit(solution)/shard_map/ppermute | solution.py:341
  56.3 8.9 %collective-permute-start.15 = (bf16[2,256,128]{2,1,0:T(8,128)(2,1)}, bf16[2,256,128]{2,1,0:T(8,128)(2,1)}, u32[]{:S(2)}, u32[]{:S(2)}) collective-permute-start(bf16[2,256,128]{2,1,0:T(8,128)(2,1)} %get-tuple-element.50), channel_id=1, source_target_pairs={{0,33},{1,32},{2,35},{3,34},{4,37},{5,36},{6,39},{7,38},{8,41},{9,... | collective-permute-start | bytes 393224 | tf_op jit(solution)/shard_map/ppermute | solution.py:341
  65.2 6.1 %collective-permute-start.16 = (bf16[2,256,128]{2,1,0:T(8,128)(2,1)}, bf16[2,256,128]{2,1,0:T(8,128)(2,1)}, u32[]{:S(2)}, u32[]{:S(2)}) collective-permute-start(bf16[2,256,128]{2,1,0:T(8,128)(2,1)} %get-tuple-element.54), channel_id=1, source_target_pairs={{0,32},{1,33},{2,34},{3,35},{4,36},{5,37},{6,38},{7,39},{8,40},{9,... | collective-permute-start | bytes 393224 | tf_op jit(solution)/shard_map/ppermute | solution.py:341
  68.1 5.9 %collective-permute-start.17 = (bf16[2,256,128]{2,1,0:T(8,128)(2,1)}, bf16[2,256,128]{2,1,0:T(8,128)(2,1)}, u32[]{:S(2)}, u32[]{:S(2)}) collective-permute-start(bf16[2,256,128]{2,1,0:T(8,128)(2,1)} %get-tuple-element.52.refs_1_), channel_id=1, source_target_pairs={{0,1},{1,0},{2,3},{3,2},{4,5},{5,4},{6,7},{7,6},{8,9},{9,8},{10,11... | collective-permute-start | bytes 393224 | tf_op jit(solution)/shard_map/ppermute | solution.py:341
  68.5 9.6 %collective-permute-start.18 = (bf16[2,256,128]{2,1,0:T(8,128)(2,1)}, bf16[2,256,128]{2,1,0:T(8,128)(2,1)}, u32[]{:S(2)}, u32[]{:S(2)}) collective-permute-start(bf16[2,256,128]{2,1,0:T(8,128)(2,1)} %get-tuple-element.54), channel_id=1, source_target_pairs={{0,33},{1,32},{2,35},{3,34},{4,37},{5,36},{6,39},{7,38},{8,41},{9,... | collective-permute-start | bytes 393224 | tf_op jit(solution)/shard_map/ppermute | solution.py:341

commit v2 on v1

--- a/solution.py
+++ b/solution.py
@@ -105,34 +105,29 @@
         copy.wait()
 
 
-def gather_kernel(kvx, kvm, ctx, four, halo, sems):
-    tm, count = lax.axis_index("tm"), lax.axis_size("tm")
-    mine = tm % 2
+def gather_kernel(kvx, kvm, four, halo, sems):
+    mine = x_low()
     pairs = [(kvm, four.at[:, pl.ds(2 * mine, 2)]), (kvx, four.at[:, pl.ds(2 - 2 * mine, 2)])]
 
-    @pl.when(tm >= count - 2)
-    def _():
-        run_copies(pairs + [(ctx, halo)], sems)
-
-    @pl.when((tm < count - 2) & (mine == 0))
+    @pl.when(mine == 0)
     def _():
         run_copies(pairs + [(kvm.at[:, 1], halo.at[:, 0]), (kvx, halo.at[:, pl.ds(1, 2)])], sems)
 
-    @pl.when((tm < count - 2) & (mine == 1))
+    @pl.when(mine == 1)
     def _():
         run_copies(pairs + [(kvx.at[:, 1], halo.at[:, 0]), (kvm, halo.at[:, pl.ds(1, 2)])], sems)
 
 
-def gather(kvx, kvm, ctx):
+def gather(kvx, kvm):
     return pl.pallas_call(
         gather_kernel,
         out_shape=[bf16(2, 4, TILE, HD), bf16(2, 3, TILE, HD)],
-        in_specs=[ANY] * 3,
+        in_specs=[ANY] * 2,
         out_specs=[VMEM] * 2,
         scratch_shapes=[pltpu.SemaphoreType.DMA((4,))],
         compiler_params=PARAMS,
         cost_estimate=SMALL,
-    )(kvx, kvm, ctx)
+    )(kvx, kvm)
 
 
 def attend_pairs(plan, count, off, bias, q, keys, values, peak, acc, bufs, at_step=None):
@@ -273,8 +268,9 @@
     rows = lambda at: pl.ds(pl.multiple_of(at, part), part)
     pairs = []
     for n, piece in enumerate(pieces):
-        held = (first, second)[n // 4]
-        pairs.append((piece, held.at[:, :, pl.ds(n % 4 * HD, HD)]))
+        kind = n % 4
+        held = (first, second)[kind // 2]
+        pairs.append((piece, held.at[:, :, pl.ds((kind % 2 * PAIR + n // 4) * HD, HD)]))
     inputs = started(pairs, [sem_a.at[i] for i in range(8)])
     weights = []
     for n in range(2):
@@ -364,21 +360,23 @@
         w3,
     )
     kvx.append(to_mate(hold(sent[1], q_own)[0]))
-    q_far = to_mate(hold(q_sent, kvx[1]))
+    q_far = to_mate(hold(q_sent, kvx[0]))
 
     four, later = [], []
     for head in range(PAIR):
-        ctx = lax.dynamic_slice_in_dim(hold(context_kv, q_own), (PAIR * x_lo + head) * HD, HD, 4)
+        one, halo = gather(kvx[head], kvm[head][0])
+        later.append(to_later(halo))
+        outer = hold(one, four[0]) if head else one
+        four.append([one, to_right(outer), to_left(outer)])
+    halo = []
+    for head in range(PAIR):
+        ctx = lax.dynamic_slice_in_dim(hold(context_kv, four[1][0]), (PAIR * x_lo + head) * HD, HD, 4)
         ctx = jnp.transpose(ctx.reshape(WMAX - 1, TILE, 2, HD), (2, 0, 1, 3))
-        one, halo = gather(kvx[head], kvm[head][0], ctx)
-        later.append(to_later(halo))
-        outer = hold(one, four[0], q_far) if head else one
-        four.append([one, to_right(outer), to_left(outer)])
-    halo = [wide(one) for one in later]
+        halo.append(wide(jnp.where(tm < 2, ctx, hold(later[head], ctx))))
 
     half = w_out.shape[1] // 2
     w_part = lax.dynamic_slice(
-        hold(w_out, four[0][0]), (core * PAIR * HD, (1 - x_hi) * half), (PAIR * HD, half)
+        hold(w_out, four[0]), (core * PAIR * HD, (1 - x_hi) * half), (PAIR * HD, half)
     )
     w_mine = to_diag(w_part)
 
@@ -390,8 +388,7 @@
         else:
             mine, mates, pieces = lax.optimization_barrier((mine, mates, pieces))
         pieces.append([mine, to_mate(mates), to_over(mine), to_diag(mates)])
-    attended = [piece for both in zip(*pieces) for piece in both]
-    out = mix(attended, w_out, w_mine, w_core)
+    out = mix(pieces[0] + pieces[1], w_out, w_mine, w_core)
     return out.reshape(frames, cols, row_count, -1)
 
 

time: 83.3 us -> 77.5 us (0.930)
  waiting for transfers between devices: 13.7 us -> 8.38 us
  starting transfers between devices: 29.8 us -> 32.6 us
  local copies, waits for them, and re-layouts: 7.17 us -> 4.74 us
  Pallas kernels: 31.7 us -> 30.5 us
  other arithmetic: 0 us -> 0.9 us
    ppermute x21, waiting for transfers between devices: 13.7 us -> 8.38 us  [moved(): return lambda shard: lax.ppermute(shard, AXES, pairs)]
    dynamic_slice x4, local copies, waits for them, and re-layouts: 7.17 us -> 3.97 us  [the longest x3 2.08 us: body(): lax.dynamic_slice_in_dim(hold(context_kv, four[1][0]), (PAIR * x_lo + hea...]
    ppermute x21, starting transfers between devices: 29.8 us -> 32.6 us  [moved(): return lambda shard: lax.ppermute(shard, AXES, pairs)]
    pallas_call x2, Pallas kernels: 13.8 us -> 12.5 us  [attend(): pl.pallas_call(functools.partial(attend_kernel, head), out_shape=[bf16(2,...]
    select_n x0 -> x2, other arithmetic: none -> 0.9 us  [body(): halo.append(wide(jnp.where(tm < 2, ctx, hold(later[head], ctx))))]
  transfers between devices with their start and end apart: 21 -> 21, of which waited for: 6 -> 3; matrix products, arithmetic and copies ran while one was open for 9% -> 6% of each run, Pallas kernels for 29% -> 29%
where the time goes in v2:
time: 77.5 us; the launch traced here: 77.4 us
  starting transfers between devices  32.6 us (42%)
  Pallas kernels  30.5 us (39%)
  waiting for transfers between devices  8.38 us (11%)
  local copies, waits for them, and re-layouts  4.74 us (6%)
  other arithmetic  0.9 us (1%)
    ppermute x21, starting transfers between devices, moved(): return lambda shard: lax.ppermute(shard, AXES, pairs)  32.6 us
    pallas_call x2, Pallas kernels, attend(): pl.pallas_call(functools.partial(attend_kernel, head), out_shape=[bf16(2,...  12.5 us
    pallas_call x2, Pallas kernels, project(): pl.pallas_call(functools.partial(project_kernel, blocks, chunks), out_sha...  9.44 us
    ppermute x21, waiting for transfers between devices, moved(): return lambda shard: lax.ppermute(shard, AXES, pairs)  8.38 us
    pallas_call x1, Pallas kernels, mix(): pl.pallas_call(mix_kernel, out_shape=bf16(rows, width), in_specs=[ANY] *...  4.27 us
    pallas_call x2, Pallas kernels, gather(): pl.pallas_call(gather_kernel, out_shape=[bf16(2, 4, TILE, HD), bf16(2, 3,...  4.23 us
    dynamic_slice x3, local copies, waits for them, and re-layouts, body(): lax.dynamic_slice_in_dim(hold(context_kv, four[1][0]), (PAIR * x_lo + hea...  2.08 us
    dynamic_slice x1, local copies, waits for them, and re-layouts, body(): lax.dynamic_slice(hold(w_out, four[0]), (core * PAIR * HD, (1 - x_hi) * h...  1.89 us
  transfers between devices with their start and end apart: 21, of which 3 were waited for; matrix products, arithmetic and copies ran while one was open for 6% of the time, Pallas kernels for 29%

profile of v2, /device:TPU:1, one launch (start us, length us, event | category | flops | bytes accessed | tf_op | source)
XLA Modules:
  0.0 77.4 jit_solution(1894479569157982613)
XLA Ops:
  0.0 3.8 %shard_map.64 = (bf16[1,2,2,256,128]{4,3,2,1,0:T(8,128)(2,1)}, bf16[1,2,2,256,128]{4,3,2,1,0:T(8,128)(2,1)}) custom-call(bf16[512,2048]{1,0:T(8,128)(2,1)} %bitcast.17, bf16[3,2048,512]{2,1,0:T(8,128)(2,1)} %bitcast.15), custom_call_target="tpu_custom_call" | custom-call | flops 1000000000 | bytes 1000 | tf_op jit(solution)/shard_map/pallas_call | solution.py:84
  3.8 2.1 %collective-permute-start = (bf16[2,2,256,128]{3,2,1,0:T(8,128)(2,1)}, bf16[2,2,256,128]{3,2,1,0:T(8,128)(2,1)}, u32[]{:S(2)}, u32[]{:S(2)}) collective-permute-start(bf16[2,2,256,128]{3,2,1,0:T(8,128)(2,1)} %bitcast.22), channel_id=1, source_target_pairs={{0,32},{1,33},{2,34},{3,35},{4,36},{5,37},{6,38},{7,39},{8,40},{9,... | collective-permute-start | bytes 786440 | tf_op jit(solution)/shard_map/ppermute | solution.py:337
  5.9 5.7 %shard_map.65 = (bf16[1,2,2,256,128]{4,3,2,1,0:T(8,128)(2,1)}, bf16[1,2,2,256,128]{4,3,2,1,0:T(8,128)(2,1)}, bf16[2,2,256,128]{3,2,1,0:T(8,128)(2,1)}, bf16[2,2,256,128]{3,2,1,0:T(8,128)(2,1)}) custom-call(bf16[512,2048]{1,0:T(8,128)(2,1)} %bitcast.18, bf16[3,2048,512]{2,1,0:T(8,128)(2,1)} %bitcast.16), custom_call_target="tpu_custom_call" | custom-call | flops 1000000000 | bytes 1000 | tf_op jit(solution)/shard_map/pallas_call | solution.py:84
  11.7 2.1 %shard_map.67 = (bf16[2,4,256,128]{3,2,1,0:T(8,128)(2,1)}, bf16[2,3,256,128]{3,2,1,0:T(8,128)(2,1)}) custom-call(bf16[2,2,256,128]{3,2,1,0:T(8,128)(2,1)} %collective-permute-done.kvx, bf16[2,2,256,128]{3,2,1,0:T(8,128)(2,1)} %bitcast.21), custom_call_target="tpu_custom_call" | custom-call | flops 1000000000 | bytes 1000 | tf_op jit(solution)/shard_map/pallas_call | solution.py:122
  13.8 1.9 %collective-permute-start.10 = (bf16[2,3,256,128]{3,2,1,0:T(8,128)(2,1)}, bf16[2,3,256,128]{3,2,1,0:T(8,128)(2,1)}, u32[]{:S(2)}, u32[]{:S(2)}) collective-permute-start(bf16[2,3,256,128]{3,2,1,0:T(8,128)(2,1)} %get-tuple-element.51), channel_id=1, source_target_pairs={{0,64},{1,65},{2,66},{3,67},{4,68},{5,69},{6,70},{7,71},{8,72},{9,... | collective-permute-start | bytes 1179656 | tf_op jit(solution)/shard_map/ppermute | solution.py:337
  15.7 1.8 %collective-permute-start.4 = (bf16[2,4,256,128]{3,2,1,0:T(8,128)(2,1)}, bf16[2,4,256,128]{3,2,1,0:T(8,128)(2,1)}, u32[]{:S(2)}, u32[]{:S(2)}) collective-permute-start(bf16[2,4,256,128]{3,2,1,0:T(8,128)(2,1)} %get-tuple-element.44.refs_0_), channel_id=1, source_target_pairs={{0,30},{1,31},{2,0},{3,1},{4,2},{5,3},{6,4},{7,5},{8,6},{9,7},{10,... | collective-permute-start | bytes 1572872 | tf_op jit(solution)/shard_map/ppermute | solution.py:337
  17.5 1.5 %collective-permute-start.3 = (bf16[2,4,256,128]{3,2,1,0:T(8,128)(2,1)}, bf16[2,4,256,128]{3,2,1,0:T(8,128)(2,1)}, u32[]{:S(2)}, u32[]{:S(2)}) collective-permute-start(bf16[2,4,256,128]{3,2,1,0:T(8,128)(2,1)} %get-tuple-element.44.refs_0_), channel_id=1, source_target_pairs={{0,2},{1,3},{2,4},{3,5},{4,6},{5,7},{6,8},{7,9},{8,10},{9,11},{10,... | collective-permute-start | bytes 1572872 | tf_op jit(solution)/shard_map/ppermute | solution.py:337
  20.3 2.1 %shard_map.66 = (bf16[2,4,256,128]{3,2,1,0:T(8,128)(2,1)}, bf16[2,3,256,128]{3,2,1,0:T(8,128)(2,1)}) custom-call(bf16[2,2,256,128]{3,2,1,0:T(8,128)(2,1)} %collective-permute-done.2.kvx, bf16[2,2,256,128]{3,2,1,0:T(8,128)(2,1)} %bitcast.20), custom_call_target="tpu_custom_call" | custom-call | flops 1000000000 | bytes 1000 | tf_op jit(solution)/shard_map/pallas_call | solution.py:122
  22.4 1.4 %collective-permute-start.7 = (bf16[2,3,256,128]{3,2,1,0:T(8,128)(2,1)}, bf16[2,3,256,128]{3,2,1,0:T(8,128)(2,1)S(1)}, u32[]{:S(2)}, u32[]{:S(2)}) collective-permute-start(bf16[2,3,256,128]{3,2,1,0:T(8,128)(2,1)} %get-tuple-element.47), channel_id=1, source_target_pairs={{0,64},{1,65},{2,66},{3,67},{4,68},{5,69},{6,70},{7,71},{8,72},{9,... | collective-permute-start | bytes 1179656 | tf_op jit(solution)/shard_map/ppermute | solution.py:337
  23.7 2.0 %constant_dynamic-slice_fusion = (bf16[3,8,32,2,128]{4,3,2,1,0:T(2,128)(2,1)S(1)}, bf16[3,8,32,2,128]{4,3,2,1,0:T(2,128)(2,1)S(1)}) fusion(bf16[3,8,32,2,512]{4,3,2,1,0:T(2,128)(2,1)} %param.11, s32[]{:T(128)S(6)} %select_n.39, s32[]{:T(128)S(6)} %select_n.37), kind=kLoop, calls=%fused_computation.2 | loop fusion | bytes 1572872 | tf_op jit(solution)/shard_map/dynamic_slice | solution.py:373
  25.9 3.2 %collective-permute-start.12 = (bf16[2,3,256,128]{3,2,1,0:T(8,128)(2,1)S(1)}, bf16[2,3,256,128]{3,2,1,0:T(8,128)(2,1)S(1)}, u32[]{:S(2)}, u32[]{:S(2)}) collective-permute-start(bf16[2,3,256,128]{3,2,1,0:T(8,128)(2,1)S(1)} %broadcast_select_fusion.refs_3_), channel_id=1, source_target_pairs={{0,30},{1,31},{2,0},{3,1},{4,2},{5,3},{6,4},{7,5},{8,6},{9,7},{10,... | collective-permute-start | bytes 1179656 | tf_op jit(solution)/shard_map/ppermute | solution.py:337
  29.5 1.9 %dynamic_slice.11 = bf16[256,1024]{1,0:T(8,128)(2,1)} dynamic-slice(bf16[512,2048]{1,0:T(8,128)(2,1)} %refs_8_.1, s32[]{:T(128)S(6)} %select_n.42, s32[]{:T(128)S(6)} %select_n.43), dynamic_slice_sizes={256,1024} | dynamic-slice | bytes 1048580 | tf_op jit(solution)/shard_map/dynamic_slice | solution.py:378
  31.4 3.1 %collective-permute-start.19 = (bf16[256,1024]{1,0:T(8,128)(2,1)}, bf16[256,1024]{1,0:T(8,128)(2,1)}, u32[]{:S(2)}, u32[]{:S(2)}) collective-permute-start(bf16[256,1024]{1,0:T(8,128)(2,1)} %dynamic_slice.11), channel_id=1, source_target_pairs={{0,33},{1,32},{2,35},{3,34},{4,37},{5,36},{6,39},{7,38},{8,41},{9,... | collective-permute-start | bytes 1572872 | tf_op jit(solution)/shard_map/ppermute | solution.py:337
  34.6 1.9 %collective-permute-start.6 = (bf16[2,4,256,128]{3,2,1,0:T(8,128)(2,1)}, bf16[2,4,256,128]{3,2,1,0:T(8,128)(2,1)}, u32[]{:S(2)}, u32[]{:S(2)}) collective-permute-start(bf16[2,4,256,128]{3,2,1,0:T(8,128)(2,1)} %get-tuple-element.45.refs_0_), channel_id=1, source_target_pairs={{0,30},{1,31},{2,0},{3,1},{4,2},{5,3},{6,4},{7,5},{8,6},{9,7},{10,... | collective-permute-start | bytes 1572872 | tf_op jit(solution)/shard_map/ppermute | solution.py:337
  38.2 3.3 %collective-permute-start.9 = (bf16[2,3,256,128]{3,2,1,0:T(8,128)(2,1)}, bf16[2,3,256,128]{3,2,1,0:T(8,128)(2,1)}, u32[]{:S(2)}, u32[]{:S(2)}) collective-permute-start(bf16[2,3,256,128]{3,2,1,0:T(8,128)(2,1)} %broadcast_select_fusion.1.refs_3_), channel_id=1, source_target_pairs={{0,30},{1,31},{2,0},{3,1},{4,2},{5,3},{6,4},{7,5},{8,6},{9,7},{10,... | collective-permute-start | bytes 1179656 | tf_op jit(solution)/shard_map/ppermute | solution.py:337
  42.3 7.5 %shard_map.69 = (bf16[2,256,128]{2,1,0:T(8,128)(2,1)}, bf16[2,256,128]{2,1,0:T(8,128)(2,1)}) custom-call(s32[4]{0:T(128)} %windows.3, s32[16]{0:T(128)} %edges.3, bf16[2,2,256,128]{3,2,1,0:T(8,128)(2,1)} %get-tuple-element.37.q_own, bf16[2,2,256,128]{3,2,1,0:T(8,128)(2,1)} %collective-permute-done.1.q_far, ...), custom_call_target="tpu_custom_call" | custom-call | flops 1000000000 | bytes 1000 | tf_op jit(solution)/shard_map/pallas_call | solution.py:238
  49.8 3.0 %collective-permute-start.20 = (bf16[256,1024]{1,0:T(8,128)(2,1)}, bf16[256,1024]{1,0:T(8,128)(2,1)}, u32[]{:S(2)}, u32[]{:S(2)}) collective-permute-start(bf16[256,1024]{1,0:T(8,128)(2,1)} %collective-permute-done.19.refs_9_), channel_id=1, source_target_pairs={{0,2},{1,3},{2,0},{3,1},{4,6},{5,7},{6,4},{7,5},{8,10},{9,11},{10,... | collective-permute-start | bytes 1572872 | tf_op jit(solution)/shard_map/ppermute | solution.py:337
  52.8 3.5 %collective-permute-start.13 = (bf16[2,256,128]{2,1,0:T(8,128)(2,1)}, bf16[2,256,128]{2,1,0:T(8,128)(2,1)}, u32[]{:S(2)}, u32[]{:S(2)}) collective-permute-start(bf16[2,256,128]{2,1,0:T(8,128)(2,1)} %get-tuple-element.54), channel_id=1, source_target_pairs={{0,32},{1,33},{2,34},{3,35},{4,36},{5,37},{6,38},{7,39},{8,40},{9,... | collective-permute-start | bytes 393224 | tf_op jit(solution)/shard_map/ppermute | solution.py:337
  56.8 5.0 %shard_map.68 = (bf16[2,256,128]{2,1,0:T(8,128)(2,1)}, bf16[2,256,128]{2,1,0:T(8,128)(2,1)}) custom-call(s32[4]{0:T(128)} %windows.3, s32[16]{0:T(128)} %edges.3, bf16[2,2,256,128]{3,2,1,0:T(8,128)(2,1)} %get-tuple-element.37.q_own, bf16[2,2,256,128]{3,2,1,0:T(8,128)(2,1)} %collective-permute-done.1.q_far, ...), custom_call_target="tpu_custom_call" | custom-call | flops 1000000000 | bytes 1000 | tf_op jit(solution)/shard_map/pallas_call | solution.py:238
  61.8 1.7 %collective-permute-done.14.refs_2_ = bf16[2,256,128]{2,1,0:T(8,128)(2,1)} collective-permute-done((bf16[2,256,128]{2,1,0:T(8,128)(2,1)}, bf16[2,256,128]{2,1,0:T(8,128)(2,1)}, u32[]{:S(2)}, u32[]{:S(2)}) %collective-permute-start.14) | collective-permute-done | bytes 131104 | tf_op jit(solution)/shard_map/ppermute | solution.py:337
  63.6 2.1 %collective-permute-start.17 = (bf16[2,256,128]{2,1,0:T(8,128)(2,1)}, bf16[2,256,128]{2,1,0:T(8,128)(2,1)}, u32[]{:S(2)}, u32[]{:S(2)}) collective-permute-start(bf16[2,256,128]{2,1,0:T(8,128)(2,1)} %get-tuple-element.59.refs_4_), channel_id=1, source_target_pairs={{0,1},{1,0},{2,3},{3,2},{4,5},{5,4},{6,7},{7,6},{8,9},{9,8},{10,11... | collective-permute-start | bytes 393224 | tf_op jit(solution)/shard_map/ppermute | solution.py:337
  66.4 2.8 %collective-permute-done.17.refs_6_ = bf16[2,256,128]{2,1,0:T(8,128)(2,1)} collective-permute-done((bf16[2,256,128]{2,1,0:T(8,128)(2,1)}, bf16[2,256,128]{2,1,0:T(8,128)(2,1)}, u32[]{:S(2)}, u32[]{:S(2)}) %collective-permute-start.17) | collective-permute-done | bytes 131104 | tf_op jit(solution)/shard_map/ppermute | solution.py:337
  69.2 3.8 %collective-permute-done.18.refs_7_ = bf16[2,256,128]{2,1,0:T(8,128)(2,1)} collective-permute-done((bf16[2,256,128]{2,1,0:T(8,128)(2,1)}, bf16[2,256,128]{2,1,0:T(8,128)(2,1)}, u32[]{:S(2)}, u32[]{:S(2)}) %collective-permute-start.18) | collective-permute-done | bytes 131104 | tf_op jit(solution)/shard_map/ppermute | solution.py:337
  73.0 4.3 %shard_map.70 = bf16[512,1024]{1,0:T(8,128)(2,1)} custom-call(bf16[2,256,128]{2,1,0:T(8,128)(2,1)} %get-tuple-element.55.refs_0_, bf16[2,256,128]{2,1,0:T(8,128)(2,1)} %collective-permute-done.13.refs_1_, bf16[2,256,128]{2,1,0:T(8,128)(2,1)} %collective-permute-done.14.refs_2_, bf16[2,256,128]{2,1,0:T(8,128)(2,1)} %collective-permute-done.15.refs_3_, ...), custom_call_target="tpu_custom_call" | custom-call | flops 1000000000 | bytes 1000 | tf_op jit(solution)/shard_map/pallas_call | solution.py:309
  (37 shorter events, 5.6 us)
Async XLA Ops:
  3.8 7.9 %collective-permute-start = (bf16[2,2,256,128]{3,2,1,0:T(8,128)(2,1)}, bf16[2,2,256,128]{3,2,1,0:T(8,128)(2,1)}, u32[]{:S(2)}, u32[]{:S(2)}) collective-permute-start(bf16[2,2,256,128]{3,2,1,0:T(8,128)(2,1)} %bitcast.22), channel_id=1, source_target_pairs={{0,32},{1,33},{2,34},{3,35},{4,36},{5,37},{6,38},{7,39},{8,40},{9,... | collective-permute-start | bytes 786440 | tf_op jit(solution)/shard_map/ppermute | solution.py:337
  11.6 8.7 %collective-permute-start.2 = (bf16[2,2,256,128]{3,2,1,0:T(8,128)(2,1)}, bf16[2,2,256,128]{3,2,1,0:T(8,128)(2,1)}, u32[]{:S(2)}, u32[]{:S(2)}) collective-permute-start(bf16[2,2,256,128]{3,2,1,0:T(8,128)(2,1)} %bitcast.19), channel_id=1, source_target_pairs={{0,32},{1,33},{2,34},{3,35},{4,36},{5,37},{6,38},{7,39},{8,40},{9,... | collective-permute-start | bytes 786440 | tf_op jit(solution)/shard_map/ppermute | solution.py:337
  13.8 12.0 %collective-permute-start.10 = (bf16[2,3,256,128]{3,2,1,0:T(8,128)(2,1)}, bf16[2,3,256,128]{3,2,1,0:T(8,128)(2,1)}, u32[]{:S(2)}, u32[]{:S(2)}) collective-permute-start(bf16[2,3,256,128]{3,2,1,0:T(8,128)(2,1)} %get-tuple-element.51), channel_id=1, source_target_pairs={{0,64},{1,65},{2,66},{3,67},{4,68},{5,69},{6,70},{7,71},{8,72},{9,... | collective-permute-start | bytes 1179656 | tf_op jit(solution)/shard_map/ppermute | solution.py:337
  15.7 13.4 %collective-permute-start.4 = (bf16[2,4,256,128]{3,2,1,0:T(8,128)(2,1)}, bf16[2,4,256,128]{3,2,1,0:T(8,128)(2,1)}, u32[]{:S(2)}, u32[]{:S(2)}) collective-permute-start(bf16[2,4,256,128]{3,2,1,0:T(8,128)(2,1)} %get-tuple-element.44.refs_0_), channel_id=1, source_target_pairs={{0,30},{1,31},{2,0},{3,1},{4,2},{5,3},{6,4},{7,5},{8,6},{9,7},{10,... | collective-permute-start | bytes 1572872 | tf_op jit(solution)/shard_map/ppermute | solution.py:337
  17.5 12.0 %collective-permute-start.3 = (bf16[2,4,256,128]{3,2,1,0:T(8,128)(2,1)}, bf16[2,4,256,128]{3,2,1,0:T(8,128)(2,1)}, u32[]{:S(2)}, u32[]{:S(2)}) collective-permute-start(bf16[2,4,256,128]{3,2,1,0:T(8,128)(2,1)} %get-tuple-element.44.refs_0_), channel_id=1, source_target_pairs={{0,2},{1,3},{2,4},{3,5},{4,6},{5,7},{6,8},{7,9},{8,10},{9,11},{10,... | collective-permute-start | bytes 1572872 | tf_op jit(solution)/shard_map/ppermute | solution.py:337
  19.0 17.5 %collective-permute-start.1 = (bf16[2,2,256,128]{3,2,1,0:T(8,128)(2,1)}, bf16[2,2,256,128]{3,2,1,0:T(8,128)(2,1)}, u32[]{:S(2)}, u32[]{:S(2)}) collective-permute-start(bf16[2,2,256,128]{3,2,1,0:T(8,128)(2,1)} %get-tuple-element.39), channel_id=1, source_target_pairs={{0,32},{1,33},{2,34},{3,35},{4,36},{5,37},{6,38},{7,39},{8,40},{9,... | collective-permute-start | bytes 786440 | tf_op jit(solution)/shard_map/ppermute | solution.py:337
  22.4 12.3 %collective-permute-start.7 = (bf16[2,3,256,128]{3,2,1,0:T(8,128)(2,1)}, bf16[2,3,256,128]{3,2,1,0:T(8,128)(2,1)S(1)}, u32[]{:S(2)}, u32[]{:S(2)}) collective-permute-start(bf16[2,3,256,128]{3,2,1,0:T(8,128)(2,1)} %get-tuple-element.47), channel_id=1, source_target_pairs={{0,64},{1,65},{2,66},{3,67},{4,68},{5,69},{6,70},{7,71},{8,72},{9,... | collective-permute-start | bytes 1179656 | tf_op jit(solution)/shard_map/ppermute | solution.py:337
  25.9 12.3 %copy-start = (bf16[2,3,256,128]{3,2,1,0:T(8,128)(2,1)}, bf16[2,3,256,128]{3,2,1,0:T(8,128)(2,1)S(1)}, u32[]{:S(2)}) copy-start(bf16[2,3,256,128]{3,2,1,0:T(8,128)(2,1)S(1)} %broadcast_select_fusion.refs_3_) | copy-start | bytes 1179652
  25.9 12.3 %collective-permute-start.12 = (bf16[2,3,256,128]{3,2,1,0:T(8,128)(2,1)S(1)}, bf16[2,3,256,128]{3,2,1,0:T(8,128)(2,1)S(1)}, u32[]{:S(2)}, u32[]{:S(2)}) collective-permute-start(bf16[2,3,256,128]{3,2,1,0:T(8,128)(2,1)S(1)} %broadcast_select_fusion.refs_3_), channel_id=1, source_target_pairs={{0,30},{1,31},{2,0},{3,1},{4,2},{5,3},{6,4},{7,5},{8,6},{9,7},{10,... | collective-permute-start | bytes 1179656 | tf_op jit(solution)/shard_map/ppermute | solution.py:337
  29.1 12.4 %collective-permute-start.11 = (bf16[2,3,256,128]{3,2,1,0:T(8,128)(2,1)S(1)}, bf16[2,3,256,128]{3,2,1,0:T(8,128)(2,1)S(1)}, u32[]{:S(2)}, u32[]{:S(2)}) collective-permute-start(bf16[2,3,256,128]{3,2,1,0:T(8,128)(2,1)S(1)} %broadcast_select_fusion.refs_3_), channel_id=1, source_target_pairs={{0,2},{1,3},{2,4},{3,5},{4,6},{5,7},{6,8},{7,9},{8,10},{9,11},{10,... | collective-permute-start | bytes 1179656 | tf_op jit(solution)/shard_map/ppermute | solution.py:337
  31.4 18.3 %collective-permute-start.19 = (bf16[256,1024]{1,0:T(8,128)(2,1)}, bf16[256,1024]{1,0:T(8,128)(2,1)}, u32[]{:S(2)}, u32[]{:S(2)}) collective-permute-start(bf16[256,1024]{1,0:T(8,128)(2,1)} %dynamic_slice.11), channel_id=1, source_target_pairs={{0,33},{1,32},{2,35},{3,34},{4,37},{5,36},{6,39},{7,38},{8,41},{9,... | collective-permute-start | bytes 1572872 | tf_op jit(solution)/shard_map/ppermute | solution.py:337
  34.6 21.6 %collective-permute-start.6 = (bf16[2,4,256,128]{3,2,1,0:T(8,128)(2,1)}, bf16[2,4,256,128]{3,2,1,0:T(8,128)(2,1)}, u32[]{:S(2)}, u32[]{:S(2)}) collective-permute-start(bf16[2,4,256,128]{3,2,1,0:T(8,128)(2,1)} %get-tuple-element.45.refs_0_), channel_id=1, source_target_pairs={{0,30},{1,31},{2,0},{3,1},{4,2},{5,3},{6,4},{7,5},{8,6},{9,7},{10,... | collective-permute-start | bytes 1572872 | tf_op jit(solution)/shard_map/ppermute | solution.py:337
  36.5 20.2 %collective-permute-start.5 = (bf16[2,4,256,128]{3,2,1,0:T(8,128)(2,1)}, bf16[2,4,256,128]{3,2,1,0:T(8,128)(2,1)}, u32[]{:S(2)}, u32[]{:S(2)}) collective-permute-start(bf16[2,4,256,128]{3,2,1,0:T(8,128)(2,1)} %get-tuple-element.45.refs_0_), channel_id=1, source_target_pairs={{0,2},{1,3},{2,4},{3,5},{4,6},{5,7},{6,8},{7,9},{8,10},{9,11},{10,... | collective-permute-start | bytes 1572872 | tf_op jit(solution)/shard_map/ppermute | solution.py:337
  38.2 3.3 %copy-start.1 = (bf16[2,3,256,128]{3,2,1,0:T(8,128)(2,1)}, bf16[2,3,256,128]{3,2,1,0:T(8,128)(2,1)S(1)}, u32[]{:S(2)}) copy-start(bf16[2,3,256,128]{3,2,1,0:T(8,128)(2,1)S(1)} %collective-permute-done.12.refs_5_) | copy-start | bytes 1179652
  38.2 14.6 %collective-permute-start.9 = (bf16[2,3,256,128]{3,2,1,0:T(8,128)(2,1)}, bf16[2,3,256,128]{3,2,1,0:T(8,128)(2,1)}, u32[]{:S(2)}, u32[]{:S(2)}) collective-permute-start(bf16[2,3,256,128]{3,2,1,0:T(8,128)(2,1)} %broadcast_select_fusion.1.refs_3_), channel_id=1, source_target_pairs={{0,30},{1,31},{2,0},{3,1},{4,2},{5,3},{6,4},{7,5},{8,6},{9,7},{10,... | collective-permute-start | bytes 1179656 | tf_op jit(solution)/shard_map/ppermute | solution.py:337
  41.5 0.8 copy-start.2
  42.3 10.6 %collective-permute-start.8 = (bf16[2,3,256,128]{3,2,1,0:T(8,128)(2,1)}, bf16[2,3,256,128]{3,2,1,0:T(8,128)(2,1)}, u32[]{:S(2)}, u32[]{:S(2)}) collective-permute-start(bf16[2,3,256,128]{3,2,1,0:T(8,128)(2,1)} %broadcast_select_fusion.1.refs_3_), channel_id=1, source_target_pairs={{0,2},{1,3},{2,4},{3,5},{4,6},{5,7},{6,8},{7,9},{8,10},{9,11},{10,... | collective-permute-start | bytes 1179656 | tf_op jit(solution)/shard_map/ppermute | solution.py:337
  49.8 23.2 %collective-permute-start.20 = (bf16[256,1024]{1,0:T(8,128)(2,1)}, bf16[256,1024]{1,0:T(8,128)(2,1)}, u32[]{:S(2)}, u32[]{:S(2)}) collective-permute-start(bf16[256,1024]{1,0:T(8,128)(2,1)} %collective-permute-done.19.refs_9_), channel_id=1, source_target_pairs={{0,2},{1,3},{2,0},{3,1},{4,6},{5,7},{6,4},{7,5},{8,10},{9,11},{10,... | collective-permute-start | bytes 1572872 | tf_op jit(solution)/shard_map/ppermute | solution.py:337
  52.8 9.0 %collective-permute-start.15 = (bf16[2,256,128]{2,1,0:T(8,128)(2,1)}, bf16[2,256,128]{2,1,0:T(8,128)(2,1)}, u32[]{:S(2)}, u32[]{:S(2)}) collective-permute-start(bf16[2,256,128]{2,1,0:T(8,128)(2,1)} %get-tuple-element.54), channel_id=1, source_target_pairs={{0,33},{1,32},{2,35},{3,34},{4,37},{5,36},{6,39},{7,38},{8,41},{9,... | collective-permute-start | bytes 393224 | tf_op jit(solution)/shard_map/ppermute | solution.py:337
  52.8 9.0 %collective-permute-start.13 = (bf16[2,256,128]{2,1,0:T(8,128)(2,1)}, bf16[2,256,128]{2,1,0:T(8,128)(2,1)}, u32[]{:S(2)}, u32[]{:S(2)}) collective-permute-start(bf16[2,256,128]{2,1,0:T(8,128)(2,1)} %get-tuple-element.54), channel_id=1, source_target_pairs={{0,32},{1,33},{2,34},{3,35},{4,36},{5,37},{6,38},{7,39},{8,40},{9,... | collective-permute-start | bytes 393224 | tf_op jit(solution)/shard_map/ppermute | solution.py:337
  56.3 7.3 %collective-permute-start.14 = (bf16[2,256,128]{2,1,0:T(8,128)(2,1)}, bf16[2,256,128]{2,1,0:T(8,128)(2,1)}, u32[]{:S(2)}, u32[]{:S(2)}) collective-permute-start(bf16[2,256,128]{2,1,0:T(8,128)(2,1)} %get-tuple-element.55.refs_0_), channel_id=1, source_target_pairs={{0,1},{1,0},{2,3},{3,2},{4,5},{5,4},{6,7},{7,6},{8,9},{9,8},{10,11... | collective-permute-start | bytes 393224 | tf_op jit(solution)/shard_map/ppermute | solution.py:337
  63.6 5.6 %collective-permute-start.17 = (bf16[2,256,128]{2,1,0:T(8,128)(2,1)}, bf16[2,256,128]{2,1,0:T(8,128)(2,1)}, u32[]{:S(2)}, u32[]{:S(2)}) collective-permute-start(bf16[2,256,128]{2,1,0:T(8,128)(2,1)} %get-tuple-element.59.refs_4_), channel_id=1, source_target_pairs={{0,1},{1,0},{2,3},{3,2},{4,5},{5,4},{6,7},{7,6},{8,9},{9,8},{10,11... | collective-permute-start | bytes 393224 | tf_op jit(solution)/shard_map/ppermute | solution.py:337
  65.7 7.3 %collective-permute-start.18 = (bf16[2,256,128]{2,1,0:T(8,128)(2,1)}, bf16[2,256,128]{2,1,0:T(8,128)(2,1)}, u32[]{:S(2)}, u32[]{:S(2)}) collective-permute-start(bf16[2,256,128]{2,1,0:T(8,128)(2,1)} %get-tuple-element.60), channel_id=1, source_target_pairs={{0,33},{1,32},{2,35},{3,34},{4,37},{5,36},{6,39},{7,38},{8,41},{9,... | collective-permute-start | bytes 393224 | tf_op jit(solution)/shard_map/ppermute | solution.py:337
  66.4 6.6 %collective-permute-start.16 = (bf16[2,256,128]{2,1,0:T(8,128)(2,1)}, bf16[2,256,128]{2,1,0:T(8,128)(2,1)}, u32[]{:S(2)}, u32[]{:S(2)}) collective-permute-start(bf16[2,256,128]{2,1,0:T(8,128)(2,1)} %get-tuple-element.60), channel_id=1, source_target_pairs={{0,32},{1,33},{2,34},{3,35},{4,36},{5,37},{6,38},{7,39},{8,40},{9,... | collective-permute-start | bytes 393224 | tf_op jit(solution)/shard_map/ppermute | solution.py:337

commit v3 on v2

--- a/solution.py
+++ b/solution.py
@@ -213,18 +213,19 @@
         rows = pl.ds(PLACES[n % 3] * TILE, TILE)
         pairs.append((piece.at[0], keys.at[frames, rows]))
         pairs.append((piece.at[1], values.at[frames, rows, pl.ds(0, HD)]))
-    copies = started(pairs, [sems.at[i] for i in range(len(pairs))])
+    copies = started(pairs[:8], [sems.at[i] for i in range(8)])
     values[:, :, HD:] = jnp.ones((values.shape[0], 3 * TILE, HD), jnp.bfloat16)
     acc[...] = jnp.zeros_like(acc)
     peak[...] = jnp.full_like(peak, -jnp.inf)
     count = plan_pairs(windows[PAIR * mine + head], plan, off)
-    for copy in copies[:8]:
+    for copy in copies:
         copy.wait()
+    copies = started(pairs[8:], [sems.at[i] for i in range(8, len(pairs))])
 
     def earlier(j):
         @pl.when(j == 1)
         def _():
-            for copy in copies[8:]:
+            for copy in copies:
                 copy.wait()
 
     attend_pairs(plan, count, off, edge_bias(edges), q, keys, values, peak, acc, bufs, earlier)
@@ -264,7 +265,8 @@
     mine, core, head = x_low(), lax.axis_index("cam") % 2, lax.axis_index("head")
     part = PAIR * HD
     width = w.shape[1]
-    half = width // 2
+    steps = made.shape[0]
+    half = width // steps
     rows = lambda at: pl.ds(pl.multiple_of(at, part), part)
     pairs = []
     for n, piece in enumerate(pieces):
@@ -273,7 +275,7 @@
         pairs.append((piece, held.at[:, :, pl.ds((kind % 2 * PAIR + n // 4) * HD, HD)]))
     inputs = started(pairs, [sem_a.at[i] for i in range(8)])
     weights = []
-    for n in range(2):
+    for n in range(steps):
         cols = pl.ds(n * half, half)
         there = pl.ds(pl.multiple_of(head * width + n * half, half), half)
         pairs = [
@@ -293,7 +295,7 @@
         return total.astype(jnp.bfloat16).astype(jnp.float32)
 
     outs = []
-    for n in range(2):
+    for n in range(steps):
         for copy in weights[n]:
             copy.wait()
         cols = slice(n * half, (n + 1) * half)
@@ -315,10 +317,10 @@
             pltpu.VMEM((2, TILE, 2 * PAIR * HD), jnp.bfloat16),
             pltpu.VMEM((2, TILE, 2 * PAIR * HD), jnp.bfloat16),
             pltpu.VMEM((4 * PAIR * HD, width), jnp.bfloat16),
-            pltpu.VMEM((2, rows, width // 2), jnp.bfloat16),
+            pltpu.VMEM((4, rows, width // 4), jnp.bfloat16),
             pltpu.SemaphoreType.DMA((8,)),
-            pltpu.SemaphoreType.DMA((2, 4)),
-            pltpu.SemaphoreType.DMA((2,)),
+            pltpu.SemaphoreType.DMA((4, 4)),
+            pltpu.SemaphoreType.DMA((4,)),
         ],
         compiler_params=PARAMS,
         cost_estimate=SMALL,

time: 77.5 us -> 79.4 us (1.025)
  Pallas kernels: 30.5 us -> 33.7 us
  waiting for transfers between devices: 8.38 us -> 6.15 us
  starting transfers between devices: 32.6 us -> 33.8 us
    pallas_call x2, Pallas kernels: 12.5 us -> 15.3 us  [attend(): pl.pallas_call(functools.partial(attend_kernel, head), out_shape=[bf16(2,...]
    ppermute x21, waiting for transfers between devices: 8.38 us -> 6.15 us  [moved(): return lambda shard: lax.ppermute(shard, AXES, pairs)]
    ppermute x21, starting transfers between devices: 32.6 us -> 33.8 us  [moved(): return lambda shard: lax.ppermute(shard, AXES, pairs)]
  transfers between devices with their start and end apart: 21 -> 21, of which waited for: 3 -> 3; matrix products, arithmetic and copies ran while one was open for 6% -> 6% of each run, Pallas kernels for 29% -> 32%
where the time goes in v3:
time: 79.4 us; the launch traced here: 79.6 us
  starting transfers between devices  33.8 us (43%)
  Pallas kernels  33.7 us (42%)
  waiting for transfers between devices  6.15 us (8%)
  local copies, waits for them, and re-layouts  4.74 us (6%)
  other arithmetic  0.9 us (1%)
    ppermute x21, starting transfers between devices, moved(): return lambda shard: lax.ppermute(shard, AXES, pairs)  33.8 us
    pallas_call x2, Pallas kernels, attend(): pl.pallas_call(functools.partial(attend_kernel, head), out_shape=[bf16(2,...  15.3 us
    pallas_call x2, Pallas kernels, project(): pl.pallas_call(functools.partial(project_kernel, blocks, chunks), out_sha...  9.44 us
    ppermute x21, waiting for transfers between devices, moved(): return lambda shard: lax.ppermute(shard, AXES, pairs)  6.15 us
    pallas_call x1, Pallas kernels, mix(): pl.pallas_call(mix_kernel, out_shape=bf16(rows, width), in_specs=[ANY] *...  4.74 us
    pallas_call x2, Pallas kernels, gather(): pl.pallas_call(gather_kernel, out_shape=[bf16(2, 4, TILE, HD), bf16(2, 3,...  4.23 us
    dynamic_slice x3, local copies, waits for them, and re-layouts, body(): lax.dynamic_slice_in_dim(hold(context_kv, four[1][0]), (PAIR * x_lo + hea...  2.08 us
    dynamic_slice x1, local copies, waits for them, and re-layouts, body(): lax.dynamic_slice(hold(w_out, four[0]), (core * PAIR * HD, (1 - x_hi) * h...  1.89 us
  transfers between devices with their start and end apart: 21, of which 3 were waited for; matrix products, arithmetic and copies ran while one was open for 6% of the time, Pallas kernels for 32%

profile of v3, /device:TPU:1, one launch (start us, length us, event | category | flops | bytes accessed | tf_op | source)
XLA Modules:
  0.0 79.6 jit_solution(7460205248732465031)
XLA Ops:
  0.0 3.8 %shard_map.64 = (bf16[1,2,2,256,128]{4,3,2,1,0:T(8,128)(2,1)}, bf16[1,2,2,256,128]{4,3,2,1,0:T(8,128)(2,1)}) custom-call(bf16[512,2048]{1,0:T(8,128)(2,1)} %bitcast.17, bf16[3,2048,512]{2,1,0:T(8,128)(2,1)} %bitcast.15), custom_call_target="tpu_custom_call" | custom-call | flops 1000000000 | bytes 1000 | tf_op jit(solution)/shard_map/pallas_call | solution.py:84
  3.8 2.1 %collective-permute-start = (bf16[2,2,256,128]{3,2,1,0:T(8,128)(2,1)}, bf16[2,2,256,128]{3,2,1,0:T(8,128)(2,1)}, u32[]{:S(2)}, u32[]{:S(2)}) collective-permute-start(bf16[2,2,256,128]{3,2,1,0:T(8,128)(2,1)} %bitcast.22), channel_id=1, source_target_pairs={{0,32},{1,33},{2,34},{3,35},{4,36},{5,37},{6,38},{7,39},{8,40},{9,... | collective-permute-start | bytes 786440 | tf_op jit(solution)/shard_map/ppermute | solution.py:339
  5.9 5.7 %shard_map.65 = (bf16[1,2,2,256,128]{4,3,2,1,0:T(8,128)(2,1)}, bf16[1,2,2,256,128]{4,3,2,1,0:T(8,128)(2,1)}, bf16[2,2,256,128]{3,2,1,0:T(8,128)(2,1)}, bf16[2,2,256,128]{3,2,1,0:T(8,128)(2,1)}) custom-call(bf16[512,2048]{1,0:T(8,128)(2,1)} %bitcast.18, bf16[3,2048,512]{2,1,0:T(8,128)(2,1)} %bitcast.16), custom_call_target="tpu_custom_call" | custom-call | flops 1000000000 | bytes 1000 | tf_op jit(solution)/shard_map/pallas_call | solution.py:84
  11.7 2.1 %shard_map.67 = (bf16[2,4,256,128]{3,2,1,0:T(8,128)(2,1)}, bf16[2,3,256,128]{3,2,1,0:T(8,128)(2,1)}) custom-call(bf16[2,2,256,128]{3,2,1,0:T(8,128)(2,1)} %collective-permute-done.kvx, bf16[2,2,256,128]{3,2,1,0:T(8,128)(2,1)} %bitcast.21), custom_call_target="tpu_custom_call" | custom-call | flops 1000000000 | bytes 1000 | tf_op jit(solution)/shard_map/pallas_call | solution.py:122
  13.8 1.9 %collective-permute-start.10 = (bf16[2,3,256,128]{3,2,1,0:T(8,128)(2,1)}, bf16[2,3,256,128]{3,2,1,0:T(8,128)(2,1)}, u32[]{:S(2)}, u32[]{:S(2)}) collective-permute-start(bf16[2,3,256,128]{3,2,1,0:T(8,128)(2,1)} %get-tuple-element.51), channel_id=1, source_target_pairs={{0,64},{1,65},{2,66},{3,67},{4,68},{5,69},{6,70},{7,71},{8,72},{9,... | collective-permute-start | bytes 1179656 | tf_op jit(solution)/shard_map/ppermute | solution.py:339
  15.7 1.8 %collective-permute-start.4 = (bf16[2,4,256,128]{3,2,1,0:T(8,128)(2,1)}, bf16[2,4,256,128]{3,2,1,0:T(8,128)(2,1)}, u32[]{:S(2)}, u32[]{:S(2)}) collective-permute-start(bf16[2,4,256,128]{3,2,1,0:T(8,128)(2,1)} %get-tuple-element.44.refs_0_), channel_id=1, source_target_pairs={{0,30},{1,31},{2,0},{3,1},{4,2},{5,3},{6,4},{7,5},{8,6},{9,7},{10,... | collective-permute-start | bytes 1572872 | tf_op jit(solution)/shard_map/ppermute | solution.py:339
  17.5 1.5 %collective-permute-start.3 = (bf16[2,4,256,128]{3,2,1,0:T(8,128)(2,1)}, bf16[2,4,256,128]{3,2,1,0:T(8,128)(2,1)}, u32[]{:S(2)}, u32[]{:S(2)}) collective-permute-start(bf16[2,4,256,128]{3,2,1,0:T(8,128)(2,1)} %get-tuple-element.44.refs_0_), channel_id=1, source_target_pairs={{0,2},{1,3},{2,4},{3,5},{4,6},{5,7},{6,8},{7,9},{8,10},{9,11},{10,... | collective-permute-start | bytes 1572872 | tf_op jit(solution)/shard_map/ppermute | solution.py:339
  20.3 2.1 %shard_map.66 = (bf16[2,4,256,128]{3,2,1,0:T(8,128)(2,1)}, bf16[2,3,256,128]{3,2,1,0:T(8,128)(2,1)}) custom-call(bf16[2,2,256,128]{3,2,1,0:T(8,128)(2,1)} %collective-permute-done.2.kvx, bf16[2,2,256,128]{3,2,1,0:T(8,128)(2,1)} %bitcast.20), custom_call_target="tpu_custom_call" | custom-call | flops 1000000000 | bytes 1000 | tf_op jit(solution)/shard_map/pallas_call | solution.py:122
  22.4 1.4 %collective-permute-start.7 = (bf16[2,3,256,128]{3,2,1,0:T(8,128)(2,1)}, bf16[2,3,256,128]{3,2,1,0:T(8,128)(2,1)S(1)}, u32[]{:S(2)}, u32[]{:S(2)}) collective-permute-start(bf16[2,3,256,128]{3,2,1,0:T(8,128)(2,1)} %get-tuple-element.47), channel_id=1, source_target_pairs={{0,64},{1,65},{2,66},{3,67},{4,68},{5,69},{6,70},{7,71},{8,72},{9,... | collective-permute-start | bytes 1179656 | tf_op jit(solution)/shard_map/ppermute | solution.py:339
  23.7 2.0 %constant_dynamic-slice_fusion = (bf16[3,8,32,2,128]{4,3,2,1,0:T(2,128)(2,1)S(1)}, bf16[3,8,32,2,128]{4,3,2,1,0:T(2,128)(2,1)S(1)}) fusion(bf16[3,8,32,2,512]{4,3,2,1,0:T(2,128)(2,1)} %param.11, s32[]{:T(128)S(6)} %select_n.39, s32[]{:T(128)S(6)} %select_n.37), kind=kLoop, calls=%fused_computation.2 | loop fusion | bytes 1572872 | tf_op jit(solution)/shard_map/dynamic_slice | solution.py:375
  25.9 3.2 %collective-permute-start.12 = (bf16[2,3,256,128]{3,2,1,0:T(8,128)(2,1)S(1)}, bf16[2,3,256,128]{3,2,1,0:T(8,128)(2,1)S(1)}, u32[]{:S(2)}, u32[]{:S(2)}) collective-permute-start(bf16[2,3,256,128]{3,2,1,0:T(8,128)(2,1)S(1)} %broadcast_select_fusion.refs_3_), channel_id=1, source_target_pairs={{0,30},{1,31},{2,0},{3,1},{4,2},{5,3},{6,4},{7,5},{8,6},{9,7},{10,... | collective-permute-start | bytes 1179656 | tf_op jit(solution)/shard_map/ppermute | solution.py:339
  29.5 1.9 %dynamic_slice.11 = bf16[256,1024]{1,0:T(8,128)(2,1)} dynamic-slice(bf16[512,2048]{1,0:T(8,128)(2,1)} %refs_8_.1, s32[]{:T(128)S(6)} %select_n.42, s32[]{:T(128)S(6)} %select_n.43), dynamic_slice_sizes={256,1024} | dynamic-slice | bytes 1048580 | tf_op jit(solution)/shard_map/dynamic_slice | solution.py:380
  31.4 3.1 %collective-permute-start.19 = (bf16[256,1024]{1,0:T(8,128)(2,1)}, bf16[256,1024]{1,0:T(8,128)(2,1)}, u32[]{:S(2)}, u32[]{:S(2)}) collective-permute-start(bf16[256,1024]{1,0:T(8,128)(2,1)} %dynamic_slice.11), channel_id=1, source_target_pairs={{0,33},{1,32},{2,35},{3,34},{4,37},{5,36},{6,39},{7,38},{8,41},{9,... | collective-permute-start | bytes 1572872 | tf_op jit(solution)/shard_map/ppermute | solution.py:339
  34.6 1.9 %collective-permute-start.6 = (bf16[2,4,256,128]{3,2,1,0:T(8,128)(2,1)}, bf16[2,4,256,128]{3,2,1,0:T(8,128)(2,1)}, u32[]{:S(2)}, u32[]{:S(2)}) collective-permute-start(bf16[2,4,256,128]{3,2,1,0:T(8,128)(2,1)} %get-tuple-element.45.refs_0_), channel_id=1, source_target_pairs={{0,30},{1,31},{2,0},{3,1},{4,2},{5,3},{6,4},{7,5},{8,6},{9,7},{10,... | collective-permute-start | bytes 1572872 | tf_op jit(solution)/shard_map/ppermute | solution.py:339
  38.2 3.3 %collective-permute-start.9 = (bf16[2,3,256,128]{3,2,1,0:T(8,128)(2,1)}, bf16[2,3,256,128]{3,2,1,0:T(8,128)(2,1)}, u32[]{:S(2)}, u32[]{:S(2)}) collective-permute-start(bf16[2,3,256,128]{3,2,1,0:T(8,128)(2,1)} %broadcast_select_fusion.1.refs_3_), channel_id=1, source_target_pairs={{0,30},{1,31},{2,0},{3,1},{4,2},{5,3},{6,4},{7,5},{8,6},{9,7},{10,... | collective-permute-start | bytes 1179656 | tf_op jit(solution)/shard_map/ppermute | solution.py:339
  42.3 7.6 %shard_map.69 = (bf16[2,256,128]{2,1,0:T(8,128)(2,1)}, bf16[2,256,128]{2,1,0:T(8,128)(2,1)}) custom-call(s32[4]{0:T(128)} %windows.3, s32[16]{0:T(128)} %edges.3, bf16[2,2,256,128]{3,2,1,0:T(8,128)(2,1)} %get-tuple-element.37.q_own, bf16[2,2,256,128]{3,2,1,0:T(8,128)(2,1)} %collective-permute-done.1.q_far, ...), custom_call_target="tpu_custom_call" | custom-call | flops 1000000000 | bytes 1000 | tf_op jit(solution)/shard_map/pallas_call | solution.py:239
  49.9 3.0 %collective-permute-start.20 = (bf16[256,1024]{1,0:T(8,128)(2,1)}, bf16[256,1024]{1,0:T(8,128)(2,1)}, u32[]{:S(2)}, u32[]{:S(2)}) collective-permute-start(bf16[256,1024]{1,0:T(8,128)(2,1)} %collective-permute-done.19.refs_9_), channel_id=1, source_target_pairs={{0,2},{1,3},{2,0},{3,1},{4,6},{5,7},{6,4},{7,5},{8,10},{9,11},{10,... | collective-permute-start | bytes 1572872 | tf_op jit(solution)/shard_map/ppermute | solution.py:339
  53.0 1.9 %collective-permute-start.15 = (bf16[2,256,128]{2,1,0:T(8,128)(2,1)}, bf16[2,256,128]{2,1,0:T(8,128)(2,1)}, u32[]{:S(2)}, u32[]{:S(2)}) collective-permute-start(bf16[2,256,128]{2,1,0:T(8,128)(2,1)} %get-tuple-element.54), channel_id=1, source_target_pairs={{0,33},{1,32},{2,35},{3,34},{4,37},{5,36},{6,39},{7,38},{8,41},{9,... | collective-permute-start | bytes 393224 | tf_op jit(solution)/shard_map/ppermute | solution.py:339
  54.8 1.6 %collective-permute-start.13 = (bf16[2,256,128]{2,1,0:T(8,128)(2,1)}, bf16[2,256,128]{2,1,0:T(8,128)(2,1)}, u32[]{:S(2)}, u32[]{:S(2)}) collective-permute-start(bf16[2,256,128]{2,1,0:T(8,128)(2,1)} %get-tuple-element.54), channel_id=1, source_target_pairs={{0,32},{1,33},{2,34},{3,35},{4,36},{5,37},{6,38},{7,39},{8,40},{9,... | collective-permute-start | bytes 393224 | tf_op jit(solution)/shard_map/ppermute | solution.py:339
  56.9 7.6 %shard_map.68 = (bf16[2,256,128]{2,1,0:T(8,128)(2,1)}, bf16[2,256,128]{2,1,0:T(8,128)(2,1)}) custom-call(s32[4]{0:T(128)} %windows.3, s32[16]{0:T(128)} %edges.3, bf16[2,2,256,128]{3,2,1,0:T(8,128)(2,1)} %get-tuple-element.37.q_own, bf16[2,2,256,128]{3,2,1,0:T(8,128)(2,1)} %collective-permute-done.1.q_far, ...), custom_call_target="tpu_custom_call" | custom-call | flops 1000000000 | bytes 1000 | tf_op jit(solution)/shard_map/pallas_call | solution.py:239
  65.8 2.3 %collective-permute-start.18 = (bf16[2,256,128]{2,1,0:T(8,128)(2,1)}, bf16[2,256,128]{2,1,0:T(8,128)(2,1)}, u32[]{:S(2)}, u32[]{:S(2)}) collective-permute-start(bf16[2,256,128]{2,1,0:T(8,128)(2,1)} %get-tuple-element.60), channel_id=1, source_target_pairs={{0,33},{1,32},{2,35},{3,34},{4,37},{5,36},{6,39},{7,38},{8,41},{9,... | collective-permute-start | bytes 393224 | tf_op jit(solution)/shard_map/ppermute | solution.py:339
  68.6 1.8 %collective-permute-done.17.refs_6_ = bf16[2,256,128]{2,1,0:T(8,128)(2,1)} collective-permute-done((bf16[2,256,128]{2,1,0:T(8,128)(2,1)}, bf16[2,256,128]{2,1,0:T(8,128)(2,1)}, u32[]{:S(2)}, u32[]{:S(2)}) %collective-permute-start.17) | collective-permute-done | bytes 131104 | tf_op jit(solution)/shard_map/ppermute | solution.py:339
  70.4 3.7 %collective-permute-done.18.refs_7_ = bf16[2,256,128]{2,1,0:T(8,128)(2,1)} collective-permute-done((bf16[2,256,128]{2,1,0:T(8,128)(2,1)}, bf16[2,256,128]{2,1,0:T(8,128)(2,1)}, u32[]{:S(2)}, u32[]{:S(2)}) %collective-permute-start.18) | collective-permute-done | bytes 131104 | tf_op jit(solution)/shard_map/ppermute | solution.py:339
  74.7 4.7 %shard_map.70 = bf16[512,1024]{1,0:T(8,128)(2,1)} custom-call(bf16[2,256,128]{2,1,0:T(8,128)(2,1)} %get-tuple-element.55.refs_0_, bf16[2,256,128]{2,1,0:T(8,128)(2,1)} %collective-permute-done.13.refs_1_, bf16[2,256,128]{2,1,0:T(8,128)(2,1)} %collective-permute-done.14.refs_2_, bf16[2,256,128]{2,1,0:T(8,128)(2,1)} %collective-permute-done.15.refs_3_, ...), custom_call_target="tpu_custom_call" | custom-call | flops 1000000000 | bytes 1000 | tf_op jit(solution)/shard_map/pallas_call | solution.py:311
  (37 shorter events, 7.2 us)
Async XLA Ops:
  3.8 7.9 %collective-permute-start = (bf16[2,2,256,128]{3,2,1,0:T(8,128)(2,1)}, bf16[2,2,256,128]{3,2,1,0:T(8,128)(2,1)}, u32[]{:S(2)}, u32[]{:S(2)}) collective-permute-start(bf16[2,2,256,128]{3,2,1,0:T(8,128)(2,1)} %bitcast.22), channel_id=1, source_target_pairs={{0,32},{1,33},{2,34},{3,35},{4,36},{5,37},{6,38},{7,39},{8,40},{9,... | collective-permute-start | bytes 786440 | tf_op jit(solution)/shard_map/ppermute | solution.py:339
  11.6 8.7 %collective-permute-start.2 = (bf16[2,2,256,128]{3,2,1,0:T(8,128)(2,1)}, bf16[2,2,256,128]{3,2,1,0:T(8,128)(2,1)}, u32[]{:S(2)}, u32[]{:S(2)}) collective-permute-start(bf16[2,2,256,128]{3,2,1,0:T(8,128)(2,1)} %bitcast.19), channel_id=1, source_target_pairs={{0,32},{1,33},{2,34},{3,35},{4,36},{5,37},{6,38},{7,39},{8,40},{9,... | collective-permute-start | bytes 786440 | tf_op jit(solution)/shard_map/ppermute | solution.py:339
  13.8 12.0 %collective-permute-start.10 = (bf16[2,3,256,128]{3,2,1,0:T(8,128)(2,1)}, bf16[2,3,256,128]{3,2,1,0:T(8,128)(2,1)}, u32[]{:S(2)}, u32[]{:S(2)}) collective-permute-start(bf16[2,3,256,128]{3,2,1,0:T(8,128)(2,1)} %get-tuple-element.51), channel_id=1, source_target_pairs={{0,64},{1,65},{2,66},{3,67},{4,68},{5,69},{6,70},{7,71},{8,72},{9,... | collective-permute-start | bytes 1179656 | tf_op jit(solution)/shard_map/ppermute | solution.py:339
  15.7 13.4 %collective-permute-start.4 = (bf16[2,4,256,128]{3,2,1,0:T(8,128)(2,1)}, bf16[2,4,256,128]{3,2,1,0:T(8,128)(2,1)}, u32[]{:S(2)}, u32[]{:S(2)}) collective-permute-start(bf16[2,4,256,128]{3,2,1,0:T(8,128)(2,1)} %get-tuple-element.44.refs_0_), channel_id=1, source_target_pairs={{0,30},{1,31},{2,0},{3,1},{4,2},{5,3},{6,4},{7,5},{8,6},{9,7},{10,... | collective-permute-start | bytes 1572872 | tf_op jit(solution)/shard_map/ppermute | solution.py:339
  17.5 12.0 %collective-permute-start.3 = (bf16[2,4,256,128]{3,2,1,0:T(8,128)(2,1)}, bf16[2,4,256,128]{3,2,1,0:T(8,128)(2,1)}, u32[]{:S(2)}, u32[]{:S(2)}) collective-permute-start(bf16[2,4,256,128]{3,2,1,0:T(8,128)(2,1)} %get-tuple-element.44.refs_0_), channel_id=1, source_target_pairs={{0,2},{1,3},{2,4},{3,5},{4,6},{5,7},{6,8},{7,9},{8,10},{9,11},{10,... | collective-permute-start | bytes 1572872 | tf_op jit(solution)/shard_map/ppermute | solution.py:339
  19.0 17.5 %collective-permute-start.1 = (bf16[2,2,256,128]{3,2,1,0:T(8,128)(2,1)}, bf16[2,2,256,128]{3,2,1,0:T(8,128)(2,1)}, u32[]{:S(2)}, u32[]{:S(2)}) collective-permute-start(bf16[2,2,256,128]{3,2,1,0:T(8,128)(2,1)} %get-tuple-element.39), channel_id=1, source_target_pairs={{0,32},{1,33},{2,34},{3,35},{4,36},{5,37},{6,38},{7,39},{8,40},{9,... | collective-permute-start | bytes 786440 | tf_op jit(solution)/shard_map/ppermute | solution.py:339
  22.4 12.3 %collective-permute-start.7 = (bf16[2,3,256,128]{3,2,1,0:T(8,128)(2,1)}, bf16[2,3,256,128]{3,2,1,0:T(8,128)(2,1)S(1)}, u32[]{:S(2)}, u32[]{:S(2)}) collective-permute-start(bf16[2,3,256,128]{3,2,1,0:T(8,128)(2,1)} %get-tuple-element.47), channel_id=1, source_target_pairs={{0,64},{1,65},{2,66},{3,67},{4,68},{5,69},{6,70},{7,71},{8,72},{9,... | collective-permute-start | bytes 1179656 | tf_op jit(solution)/shard_map/ppermute | solution.py:339
  25.9 12.3 %copy-start = (bf16[2,3,256,128]{3,2,1,0:T(8,128)(2,1)}, bf16[2,3,256,128]{3,2,1,0:T(8,128)(2,1)S(1)}, u32[]{:S(2)}) copy-start(bf16[2,3,256,128]{3,2,1,0:T(8,128)(2,1)S(1)} %broadcast_select_fusion.refs_3_) | copy-start | bytes 1179652
  25.9 12.3 %collective-permute-start.12 = (bf16[2,3,256,128]{3,2,1,0:T(8,128)(2,1)S(1)}, bf16[2,3,256,128]{3,2,1,0:T(8,128)(2,1)S(1)}, u32[]{:S(2)}, u32[]{:S(2)}) collective-permute-start(bf16[2,3,256,128]{3,2,1,0:T(8,128)(2,1)S(1)} %broadcast_select_fusion.refs_3_), channel_id=1, source_target_pairs={{0,30},{1,31},{2,0},{3,1},{4,2},{5,3},{6,4},{7,5},{8,6},{9,7},{10,... | collective-permute-start | bytes 1179656 | tf_op jit(solution)/shard_map/ppermute | solution.py:339
  29.1 12.4 %collective-permute-start.11 = (bf16[2,3,256,128]{3,2,1,0:T(8,128)(2,1)S(1)}, bf16[2,3,256,128]{3,2,1,0:T(8,128)(2,1)S(1)}, u32[]{:S(2)}, u32[]{:S(2)}) collective-permute-start(bf16[2,3,256,128]{3,2,1,0:T(8,128)(2,1)S(1)} %broadcast_select_fusion.refs_3_), channel_id=1, source_target_pairs={{0,2},{1,3},{2,4},{3,5},{4,6},{5,7},{6,8},{7,9},{8,10},{9,11},{10,... | collective-permute-start | bytes 1179656 | tf_op jit(solution)/shard_map/ppermute | solution.py:339
  31.4 18.5 %collective-permute-start.19 = (bf16[256,1024]{1,0:T(8,128)(2,1)}, bf16[256,1024]{1,0:T(8,128)(2,1)}, u32[]{:S(2)}, u32[]{:S(2)}) collective-permute-start(bf16[256,1024]{1,0:T(8,128)(2,1)} %dynamic_slice.11), channel_id=1, source_target_pairs={{0,33},{1,32},{2,35},{3,34},{4,37},{5,36},{6,39},{7,38},{8,41},{9,... | collective-permute-start | bytes 1572872 | tf_op jit(solution)/shard_map/ppermute | solution.py:339
  34.6 21.8 %collective-permute-start.6 = (bf16[2,4,256,128]{3,2,1,0:T(8,128)(2,1)}, bf16[2,4,256,128]{3,2,1,0:T(8,128)(2,1)}, u32[]{:S(2)}, u32[]{:S(2)}) collective-permute-start(bf16[2,4,256,128]{3,2,1,0:T(8,128)(2,1)} %get-tuple-element.45.refs_0_), channel_id=1, source_target_pairs={{0,30},{1,31},{2,0},{3,1},{4,2},{5,3},{6,4},{7,5},{8,6},{9,7},{10,... | collective-permute-start | bytes 1572872 | tf_op jit(solution)/shard_map/ppermute | solution.py:339
  36.5 20.4 %collective-permute-start.5 = (bf16[2,4,256,128]{3,2,1,0:T(8,128)(2,1)}, bf16[2,4,256,128]{3,2,1,0:T(8,128)(2,1)}, u32[]{:S(2)}, u32[]{:S(2)}) collective-permute-start(bf16[2,4,256,128]{3,2,1,0:T(8,128)(2,1)} %get-tuple-element.45.refs_0_), channel_id=1, source_target_pairs={{0,2},{1,3},{2,4},{3,5},{4,6},{5,7},{6,8},{7,9},{8,10},{9,11},{10,... | collective-permute-start | bytes 1572872 | tf_op jit(solution)/shard_map/ppermute | solution.py:339
  38.2 3.3 %copy-start.1 = (bf16[2,3,256,128]{3,2,1,0:T(8,128)(2,1)}, bf16[2,3,256,128]{3,2,1,0:T(8,128)(2,1)S(1)}, u32[]{:S(2)}) copy-start(bf16[2,3,256,128]{3,2,1,0:T(8,128)(2,1)S(1)} %collective-permute-done.12.refs_5_) | copy-start | bytes 1179652
  38.2 14.8 %collective-permute-start.9 = (bf16[2,3,256,128]{3,2,1,0:T(8,128)(2,1)}, bf16[2,3,256,128]{3,2,1,0:T(8,128)(2,1)}, u32[]{:S(2)}, u32[]{:S(2)}) collective-permute-start(bf16[2,3,256,128]{3,2,1,0:T(8,128)(2,1)} %broadcast_select_fusion.1.refs_3_), channel_id=1, source_target_pairs={{0,30},{1,31},{2,0},{3,1},{4,2},{5,3},{6,4},{7,5},{8,6},{9,7},{10,... | collective-permute-start | bytes 1179656 | tf_op jit(solution)/shard_map/ppermute | solution.py:339
  41.5 0.8 copy-start.2
  42.3 12.5 %collective-permute-start.8 = (bf16[2,3,256,128]{3,2,1,0:T(8,128)(2,1)}, bf16[2,3,256,128]{3,2,1,0:T(8,128)(2,1)}, u32[]{:S(2)}, u32[]{:S(2)}) collective-permute-start(bf16[2,3,256,128]{3,2,1,0:T(8,128)(2,1)} %broadcast_select_fusion.1.refs_3_), channel_id=1, source_target_pairs={{0,2},{1,3},{2,4},{3,5},{4,6},{5,7},{6,8},{7,9},{8,10},{9,11},{10,... | collective-permute-start | bytes 1179656 | tf_op jit(solution)/shard_map/ppermute | solution.py:339
  49.9 24.8 %collective-permute-start.20 = (bf16[256,1024]{1,0:T(8,128)(2,1)}, bf16[256,1024]{1,0:T(8,128)(2,1)}, u32[]{:S(2)}, u32[]{:S(2)}) collective-permute-start(bf16[256,1024]{1,0:T(8,128)(2,1)} %collective-permute-done.19.refs_9_), channel_id=1, source_target_pairs={{0,2},{1,3},{2,0},{3,1},{4,6},{5,7},{6,4},{7,5},{8,10},{9,11},{10,... | collective-permute-start | bytes 1572872 | tf_op jit(solution)/shard_map/ppermute | solution.py:339
  53.0 11.6 %collective-permute-start.15 = (bf16[2,256,128]{2,1,0:T(8,128)(2,1)}, bf16[2,256,128]{2,1,0:T(8,128)(2,1)}, u32[]{:S(2)}, u32[]{:S(2)}) collective-permute-start(bf16[2,256,128]{2,1,0:T(8,128)(2,1)} %get-tuple-element.54), channel_id=1, source_target_pairs={{0,33},{1,32},{2,35},{3,34},{4,37},{5,36},{6,39},{7,38},{8,41},{9,... | collective-permute-start | bytes 393224 | tf_op jit(solution)/shard_map/ppermute | solution.py:339
  54.8 9.8 %collective-permute-start.13 = (bf16[2,256,128]{2,1,0:T(8,128)(2,1)}, bf16[2,256,128]{2,1,0:T(8,128)(2,1)}, u32[]{:S(2)}, u32[]{:S(2)}) collective-permute-start(bf16[2,256,128]{2,1,0:T(8,128)(2,1)} %get-tuple-element.54), channel_id=1, source_target_pairs={{0,32},{1,33},{2,34},{3,35},{4,36},{5,37},{6,38},{7,39},{8,40},{9,... | collective-permute-start | bytes 393224 | tf_op jit(solution)/shard_map/ppermute | solution.py:339
  56.4 8.2 %collective-permute-start.14 = (bf16[2,256,128]{2,1,0:T(8,128)(2,1)}, bf16[2,256,128]{2,1,0:T(8,128)(2,1)}, u32[]{:S(2)}, u32[]{:S(2)}) collective-permute-start(bf16[2,256,128]{2,1,0:T(8,128)(2,1)} %get-tuple-element.55.refs_0_), channel_id=1, source_target_pairs={{0,1},{1,0},{2,3},{3,2},{4,5},{5,4},{6,7},{7,6},{8,9},{9,8},{10,11... | collective-permute-start | bytes 393224 | tf_op jit(solution)/shard_map/ppermute | solution.py:339
  64.6 5.8 %collective-permute-start.17 = (bf16[2,256,128]{2,1,0:T(8,128)(2,1)}, bf16[2,256,128]{2,1,0:T(8,128)(2,1)}, u32[]{:S(2)}, u32[]{:S(2)}) collective-permute-start(bf16[2,256,128]{2,1,0:T(8,128)(2,1)} %get-tuple-element.59.refs_4_), channel_id=1, source_target_pairs={{0,1},{1,0},{2,3},{3,2},{4,5},{5,4},{6,7},{7,6},{8,9},{9,8},{10,11... | collective-permute-start | bytes 393224 | tf_op jit(solution)/shard_map/ppermute | solution.py:339
  65.8 8.3 %collective-permute-start.18 = (bf16[2,256,128]{2,1,0:T(8,128)(2,1)}, bf16[2,256,128]{2,1,0:T(8,128)(2,1)}, u32[]{:S(2)}, u32[]{:S(2)}) collective-permute-start(bf16[2,256,128]{2,1,0:T(8,128)(2,1)} %get-tuple-element.60), channel_id=1, source_target_pairs={{0,33},{1,32},{2,35},{3,34},{4,37},{5,36},{6,39},{7,38},{8,41},{9,... | collective-permute-start | bytes 393224 | tf_op jit(solution)/shard_map/ppermute | solution.py:339
  68.1 6.6 %collective-permute-start.16 = (bf16[2,256,128]{2,1,0:T(8,128)(2,1)}, bf16[2,256,128]{2,1,0:T(8,128)(2,1)}, u32[]{:S(2)}, u32[]{:S(2)}) collective-permute-start(bf16[2,256,128]{2,1,0:T(8,128)(2,1)} %get-tuple-element.60), channel_id=1, source_target_pairs={{0,32},{1,33},{2,34},{3,35},{4,36},{5,37},{6,38},{7,39},{8,40},{9,... | collective-permute-start | bytes 393224 | tf_op jit(solution)/shard_map/ppermute | solution.py:339
